TPU v7x, 32 devices: a whole 2x2x4 slice. The times are simulated.
32 devices in a mesh: dp: 8 (over y, x, core), tensor: 4 (over z).
Axes of the slice: x: 2, y: 2, z: 4, core: 2. Of those that a mesh axis runs over, the one named last changes fastest.
Arguments:
- layer_input: bfloat16 [8192, 1024], P(('dp', 'tensor')), may hold values from -6 to 6
- query_weight: bfloat16 [1024, 1024], P('dp', 'tensor'), may hold values from -0.1875 to 0.1875
- key_weight: bfloat16 [1024, 1024], P('dp', 'tensor'), may hold values from -0.1875 to 0.1875
- value_weight: bfloat16 [1024, 1024], P('dp', 'tensor'), may hold values from -0.1875 to 0.1875
- mixing_weight: bfloat16 [1024, 1024], P('tensor', 'dp'), may hold values from -1.5 to 1.5
- expand_weight: bfloat16 [1024, 4096], P('dp', 'tensor'), may hold values from -0.1875 to 0.1875
- shrink_weight: bfloat16 [4096, 1024], P('tensor', 'dp'), may hold values from -0.09375 to 0.09375
- query_offset: bfloat16 [1024], P('tensor'), may hold values from -3 to 3
- value_offset: bfloat16 [1024], P('tensor'), may hold values from -3 to 3
- mixing_offset: bfloat16 [1024], replicated, may hold values from -2 to 2
- expand_offset: bfloat16 [4096], P('tensor'), may hold values from -3 to 3
- shrink_offset: bfloat16 [1024], replicated, may hold values from -2 to 2
- first_gain: bfloat16 [1024], replicated, may hold values from 0.25 to 1.75
- first_shift: bfloat16 [1024], replicated, may hold values from -2 to 2
- second_gain: bfloat16 [1024], replicated, may hold values from 0.25 to 1.75
- second_shift: bfloat16 [1024], replicated, may hold values from -2 to 2
- cotangent: bfloat16 [8192, 1024], P(('dp', 'tensor')), may hold values from -6 to 6
Outputs:
- layer_output: bfloat16 [8192, 1024], P(('dp', 'tensor'))
- input_grad: float32 [8192, 1024], P(('dp', 'tensor'))
- query_grad: float32 [1024, 1024], P('dp', 'tensor')
- key_grad: float32 [1024, 1024], P('dp', 'tensor')
- value_grad: float32 [1024, 1024], P('dp', 'tensor')
- mixing_grad: float32 [1024, 1024], P('tensor', 'dp')
- expand_grad: float32 [1024, 4096], P('dp', 'tensor')
- shrink_grad: float32 [4096, 1024], P('tensor', 'dp')
- offset_query: float32 [1024], P('tensor')
- offset_value: float32 [1024], P('tensor')
- offset_mixing: float32 [1024], replicated
- offset_expand: float32 [4096], P('tensor')
- offset_shrink: float32 [1024], replicated
- gain_first: float32 [1024], replicated
- shift_first: float32 [1024], replicated
- gain_second: float32 [1024], replicated
- shift_second: float32 [1024], replicated
All inputs are finite; a program needn't handle non-finite values.
Results may differ from a plain program's by a relative error of at most 0.015.
Values may be sent and summed in bfloat16 or wider, within the bound.
A program may use at most 128 MiB of HBM per device.

v0:
```python
import jax
import jax.numpy as jnp
from jax import lax
from jax.sharding import PartitionSpec as P

HD = 64


EPSILON = 1e-05
CONTRACT_ROWS = (((0,), (0,)), ((), ()))
CONTRACT_LAST = (((1,), (1,)), ((), ()))


def layer_norm(inputs, gain, shift):
    centered = inputs - jnp.mean(inputs, axis=-1, keepdims=True)
    variance = jnp.mean(centered * centered, axis=-1, keepdims=True)
    return centered * lax.rsqrt(variance + EPSILON) * gain + shift


def product(left, right):
    return jnp.dot(left, right, preferred_element_type=jnp.float32)


def product_rows(left, right):
    return lax.dot_general(left, right, CONTRACT_ROWS, preferred_element_type=jnp.float32)


def product_last(left, right):
    return lax.dot_general(left, right, CONTRACT_LAST, preferred_element_type=jnp.float32)


def gelu_exact(argument):
    return jax.nn.gelu(argument, approximate=False)


def attend_forward(queries, key_rows, values, block_rows):
    length, heads_here, head_size = queries.shape
    block_count = length // block_rows

    def one_block(query_block):
        scores = jnp.einsum(
            "qhd,khd->hqk", query_block, key_rows, preferred_element_type=jnp.float32
        )
        largest = jnp.max(scores, axis=-1, keepdims=True)
        weights = jnp.exp(scores - largest)
        exp_total = jnp.sum(weights, axis=-1, keepdims=True)
        probs_low = (weights / exp_total).astype(jnp.bfloat16)
        mixture = jnp.einsum("hqk,khd->qhd", probs_low, values, preferred_element_type=jnp.float32)
        log_total = (largest + jnp.log(exp_total))[..., 0]
        return (mixture.astype(jnp.bfloat16), log_total)

    mixture, log_totals = lax.map(
        one_block, queries.reshape(block_count, block_rows, heads_here, head_size)
    )
    return (mixture.reshape(length, heads_here * head_size), log_totals)


def attend_backward(queries, key_rows, values, mixture_low, log_totals, block_rows):
    length, heads_here, head_size = queries.shape
    block_count = length // block_rows

    def one_block(accumulated, inputs):
        key_sum, value_sum = accumulated
        query_block, grad_block, log_block = inputs
        scores = jnp.einsum(
            "qhd,khd->hqk", query_block, key_rows, preferred_element_type=jnp.float32
        )
        probability = jnp.exp(scores - log_block[..., None])
        probs_low = probability.astype(jnp.bfloat16)
        value_sum = value_sum + jnp.einsum(
            "hqk,qhd->khd", probs_low, grad_block, preferred_element_type=jnp.float32
        )
        prob_grad = jnp.einsum(
            "qhd,khd->hqk", grad_block, values, preferred_element_type=jnp.float32
        )
        inner_sum = jnp.sum(prob_grad * probability, axis=-1, keepdims=True)
        score_low = (probability * (prob_grad - inner_sum)).astype(jnp.bfloat16)
        query_low = jnp.einsum(
            "hqk,khd->qhd", score_low, key_rows, preferred_element_type=jnp.float32
        )
        key_sum = key_sum + jnp.einsum(
            "hqk,qhd->khd", score_low, query_block, preferred_element_type=jnp.float32
        )
        return ((key_sum, value_sum), query_low.astype(jnp.bfloat16))

    zeros = jnp.zeros((length, heads_here, head_size), jnp.float32)
    blocked = (length // block_count, heads_here, head_size)
    (key_sum, value_sum), query_low = lax.scan(
        one_block,
        (zeros, zeros),
        (
            queries.reshape((block_count,) + blocked),
            mixture_low.reshape((block_count,) + blocked),
            log_totals,
        ),
    )
    width_here = heads_here * head_size
    return (
        query_low.reshape(length, width_here),
        key_sum.astype(jnp.bfloat16).reshape(length, width_here),
        value_sum.astype(jnp.bfloat16).reshape(length, width_here),
    )


def body(
    layer_input,
    query_weight,
    key_weight,
    value_weight,
    mixing_weight,
    expand_weight,
    shrink_weight,
    query_offset,
    value_offset,
    mixing_offset,
    expand_offset,
    shrink_offset,
    first_gain,
    first_shift,
    second_gain,
    second_shift,
    cotangent,
):
    local_rows = layer_input.shape[0]
    tensor_size = lax.axis_size("tensor")
    length = local_rows * tensor_size
    block_rows = min(512, length)
    heads_here = query_weight.shape[1] // HD
    scaling = HD ** (-0.5)
    head_shape = (length, heads_here, HD)
    gathered = (
        lax.all_gather(query_weight, "dp", axis=0, tiled=True),
        lax.all_gather(key_weight, "dp", axis=0, tiled=True),
        lax.all_gather(value_weight, "dp", axis=0, tiled=True),
        lax.all_gather(mixing_weight, "dp", axis=1, tiled=True),
        lax.all_gather(expand_weight, "dp", axis=0, tiled=True),
        lax.all_gather(shrink_weight, "dp", axis=1, tiled=True),
    )
    query_full, key_full, value_full, mixing_full, expand_full, shrink_full = gathered
    sequence = lax.all_gather(layer_input, "tensor", axis=0, tiled=True)
    queries = ((product(sequence, query_full) + query_offset.astype(jnp.float32)) * scaling).astype(
        jnp.bfloat16
    )
    key_rows = product(sequence, key_full).astype(jnp.bfloat16)
    values = (product(sequence, value_full) + value_offset.astype(jnp.float32)).astype(jnp.bfloat16)
    mixture, log_totals = attend_forward(
        queries.reshape(head_shape),
        key_rows.reshape(head_shape),
        values.reshape(head_shape),
        block_rows,
    )
    attended_part = lax.psum_scatter(
        product(mixture, mixing_full), "tensor", scatter_dimension=0, tiled=True
    )
    attended = layer_input.astype(jnp.float32) + attended_part + mixing_offset.astype(jnp.float32)
    first_norm, first_back = jax.vjp(
        layer_norm, attended, first_gain.astype(jnp.float32), first_shift.astype(jnp.float32)
    )
    normed = lax.all_gather(first_norm.astype(jnp.bfloat16), "tensor", axis=0, tiled=True)
    expanded = product(normed, expand_full) + expand_offset.astype(jnp.float32)
    hidden_act, gelu_back = jax.vjp(gelu_exact, expanded)
    hidden = hidden_act.astype(jnp.bfloat16)
    shrunk = lax.psum_scatter(
        product(hidden, shrink_full), "tensor", scatter_dimension=0, tiled=True
    )
    summed = first_norm + shrunk + shrink_offset.astype(jnp.float32)
    normalized, second_back = jax.vjp(
        layer_norm, summed, second_gain.astype(jnp.float32), second_shift.astype(jnp.float32)
    )
    summed_grad, gain_second, shift_second = second_back(cotangent.astype(jnp.float32))
    regathered = (
        lax.all_gather(query_weight, "dp", axis=0, tiled=True),
        lax.all_gather(key_weight, "dp", axis=0, tiled=True),
        lax.all_gather(value_weight, "dp", axis=0, tiled=True),
        lax.all_gather(mixing_weight, "dp", axis=1, tiled=True),
        lax.all_gather(expand_weight, "dp", axis=0, tiled=True),
        lax.all_gather(shrink_weight, "dp", axis=1, tiled=True),
    )
    query_back, key_back, value_back, mixing_back, expand_back, shrink_back = regathered
    branch_rows = lax.all_gather(summed_grad.astype(jnp.bfloat16), "tensor", axis=0, tiled=True)
    shrink_local = product_rows(hidden, branch_rows)
    hidden_grad = product_last(branch_rows, shrink_back)
    expanded_low = gelu_back(hidden_grad)[0].astype(jnp.bfloat16)
    expand_sum = jnp.sum(expanded_low.astype(jnp.float32), axis=0)
    expand_local = product_rows(normed, expanded_low)
    first_grad = (
        lax.psum_scatter(
            product_last(expanded_low, expand_back), "tensor", scatter_dimension=0, tiled=True
        )
        + summed_grad
    )
    shrink_sum = jnp.sum(summed_grad, axis=0)
    attended_grad, gain_first, shift_first = first_back(first_grad)
    mixing_sum = jnp.sum(attended_grad, axis=0)
    attended_rows = lax.all_gather(attended_grad.astype(jnp.bfloat16), "tensor", axis=0, tiled=True)
    mixing_local = product_rows(mixture, attended_rows)
    mixture_low = product_last(attended_rows, mixing_back).astype(jnp.bfloat16)
    query_low, key_low, value_low = attend_backward(
        queries.reshape(head_shape),
        key_rows.reshape(head_shape),
        values.reshape(head_shape),
        mixture_low,
        log_totals,
        block_rows,
    )
    query_local = product_rows(sequence, query_low) * scaling
    key_local = product_rows(sequence, key_low)
    value_local = product_rows(sequence, value_low)
    query_sum = jnp.sum(query_low.astype(jnp.float32), axis=0) * scaling
    value_sum = jnp.sum(value_low.astype(jnp.float32), axis=0)
    input_grad = (
        lax.psum_scatter(
            (
                product_last(query_low, query_back) * scaling
                + product_last(key_low, key_back)
                + product_last(value_low, value_back)
            ).astype(jnp.bfloat16),
            "tensor",
            scatter_dimension=0,
            tiled=True,
        ).astype(jnp.float32)
        + attended_grad
    )
    query_grad, key_grad, value_grad, mixing_grad, expand_grad, shrink_grad = (
        lax.psum_scatter(query_local, "dp", scatter_dimension=0, tiled=True),
        lax.psum_scatter(key_local, "dp", scatter_dimension=0, tiled=True),
        lax.psum_scatter(value_local, "dp", scatter_dimension=0, tiled=True),
        lax.psum_scatter(mixing_local, "dp", scatter_dimension=1, tiled=True),
        lax.psum_scatter(expand_local, "dp", scatter_dimension=0, tiled=True),
        lax.psum_scatter(shrink_local, "dp", scatter_dimension=1, tiled=True),
    )
    tensor_index = lax.axis_index("tensor")
    selector = (jnp.arange(tensor_size)[:, None] == tensor_index).astype(jnp.float32)

    def spread_out(vector):
        return (selector * vector[None, :]).reshape(-1)

    totals = lax.psum(
        (
            gain_first,
            shift_first,
            gain_second,
            shift_second,
            mixing_sum,
            shrink_sum,
            spread_out(query_sum),
            spread_out(value_sum),
            spread_out(expand_sum),
        ),
        ("dp", "tensor"),
    )

    def own_slice(full_vector, slice_size):
        return lax.dynamic_slice_in_dim(full_vector, tensor_index * slice_size, slice_size, 0)

    offset_query = own_slice(totals[6], query_sum.shape[0])
    offset_value = own_slice(totals[7], value_sum.shape[0])
    offset_expand = own_slice(totals[8], expand_sum.shape[0])
    return (
        normalized.astype(jnp.bfloat16),
        input_grad,
        query_grad,
        key_grad,
        value_grad,
        mixing_grad,
        expand_grad,
        shrink_grad,
        offset_query,
        offset_value,
        totals[4],
        offset_expand,
        totals[5],
        totals[0],
        totals[1],
        totals[2],
        totals[3],
    )


def solution(mesh):
    placed = (
        P(("dp", "tensor"), None),
        P("dp", "tensor"),
        P("dp", "tensor"),
        P("dp", "tensor"),
        P("tensor", "dp"),
        P("dp", "tensor"),
        P("tensor", "dp"),
        P("tensor"),
        P("tensor"),
        P(),
        P("tensor"),
        P(),
        P(),
        P(),
        P(),
        P(),
        P(("dp", "tensor"), None),
    )
    return jax.shard_map(
        body,
        mesh=mesh,
        in_specs=placed,
        out_specs=(
            P(("dp", "tensor"), None),
            P(("dp", "tensor"), None),
            P("dp", "tensor"),
            P("dp", "tensor"),
            P("dp", "tensor"),
            P("tensor", "dp"),
            P("dp", "tensor"),
            P("tensor", "dp"),
            P("tensor"),
            P("tensor"),
            P(),
            P("tensor"),
            P(),
            P(),
            P(),
            P(),
            P(),
        ),
        check_vma=False,
    )
```

profile of v0, /device:TPU:0, one launch (start us, length us, event | category | flops | bytes accessed | tf_op | source)
XLA Modules:
  0.0 861.9 jit_solution(9256710127542278501)
XLA Ops:
  10.1 11.6 %all_gather.37 = bf16[1024,256]{1,0:T(8,128)(2,1)S(1)} all-gather(bf16[128,256]{1,0:T(8,128)(2,1)} %param.22), channel_id=1, replica_groups=mesh['dp'=8,'tensor'=4] {'dp'}, dimensions={0}, use_global_device_ids=true | all-gather | bytes 589824 | tf_op jit(solution)/shard_map/all_gather | solution.py:132
  21.7 10.8 %all_gather.38 = bf16[1024,256]{1,0:T(8,128)(2,1)} all-gather(bf16[128,256]{1,0:T(8,128)(2,1)} %param.23), channel_id=1, replica_groups=mesh['dp'=8,'tensor'=4] {'dp'}, dimensions={0}, use_global_device_ids=true | all-gather | bytes 589824 | tf_op jit(solution)/shard_map/all_gather | solution.py:133
  32.5 10.8 %all_gather.39 = bf16[1024,256]{1,0:T(8,128)(2,1)} all-gather(bf16[128,256]{1,0:T(8,128)(2,1)} %param.24), channel_id=1, replica_groups=mesh['dp'=8,'tensor'=4] {'dp'}, dimensions={0}, use_global_device_ids=true | all-gather | bytes 589824 | tf_op jit(solution)/shard_map/all_gather | solution.py:134
  43.3 10.9 %all_gather.40 = bf16[256,1024]{1,0:T(8,128)(2,1)} all-gather(bf16[256,128]{1,0:T(8,128)(2,1)} %param.25), channel_id=1, replica_groups=mesh['dp'=8,'tensor'=4] {'dp'}, dimensions={1}, use_global_device_ids=true | all-gather | bytes 589824 | tf_op jit(solution)/shard_map/all_gather | solution.py:135
  54.2 4.9 all-gather.7.cloned.1.call-done
  69.0 10.2 %while.27 = (s32[]{:T(128)}, bf16[2,512,4,64]{1,3,2,0:T(8,128)(2,1)S(1)}, f32[2,4,512]{2,1,0:T(4,128)S(1)}, bf16[2,512,4,64]{1,3,2,0:T(8,128)(2,1)S(1)}, bf16[10...) while((s32[]{:T(128)}, bf16[2,512,4,64]{1,3,2,0:T(8,128)(2,1)S(1)}, ...), condition=%wide.region_3.4_spmd, body=%wide.region_0.3_spmd.sunk | while | flops 549582848 | bytes 28901500 | solution.py:52
  80.7 2.7 fusion.59
  84.1 74.9 %reduce-scatter.11.cloned.1.call-done = f32[256,1024]{1,0:T(8,128)} async-done(((f32[1024,1024]{1,0:T(8,128)}), f32[256,1024]{1,0:T(8,128)}) %reduce-scatter.11.cloned.1.call-update) | async-done | bytes 1048592 | tf_op jit(solution)/shard_map/reduce_scatter | solution.py:152
  162.7 45.3 %all-gather.9.cloned.1.call-done = bf16[1024,1024]{1,0:T(8,128)(2,1)} async-done(((bf16[256,1024]{1,0:T(8,128)(2,1)}), bf16[1024,1024]{1,0:T(8,128)(2,1)}) %all-gather.9.cloned.1.call-update) | async-done | bytes 2097168 | tf_op jit(solution)/shard_map/all_gather | solution.py:159
  208.0 14.9 %multiply_convert_fusion.1 = (bf16[1024,1024]{1,0:T(8,128)(2,1)}, f32[1024,1024]{1,0:T(8,128)}, f32[1024,1024]{1,0:T(8,128)}) fusion(f32[1024]{0:T(1024)S(1)} %convert_element_type.125, bf16[1024,1024]{1,0:T(8,128)(2,1)} %all-gather.9.cloned.1.call-done, bf16[1024,1024]{1,0:T(8,128)(2,1)} %all-gather.11.cloned.1.call-done), kind=kOutput, calls=%fused_computation.45 | convolution fusion | flops 2216689664 | bytes 14684160 | tf_op jit(solution)/shard_map/dot_general | solution.py:21
  222.9 13.9 %all-gather.13.cloned.1.call-done = bf16[1024,1024]{1,0:T(8,128)(2,1)} async-done(((bf16[1024,128]{1,0:T(8,128)(2,1)}), bf16[1024,1024]{1,0:T(8,128)(2,1)}) %all-gather.13.cloned.1.call-update) | async-done | bytes 2097168 | tf_op jit(solution)/shard_map/all_gather | solution.py:137
  236.7 6.5 fusion.60
  244.0 76.2 %reduce-scatter.13.cloned.1.call-done = f32[256,1024]{1,0:T(8,128)} async-done(((f32[1024,1024]{1,0:T(8,128)}), f32[256,1024]{1,0:T(8,128)}) %reduce-scatter.13.cloned.1.call-update) | async-done | bytes 1048592 | tf_op jit(solution)/shard_map/reduce_scatter | solution.py:163
  325.9 46.5 %all-gather.15.cloned.1.call-done = bf16[1024,1024]{1,0:T(8,128)(2,1)} async-done(((bf16[256,1024]{1,0:T(8,128)(2,1)}), bf16[1024,1024]{1,0:T(8,128)(2,1)}) %all-gather.15.cloned.1.call-update) | async-done | bytes 2097168 | tf_op jit(solution)/shard_map/all_gather | solution.py:180
  372.3 8.5 convert_reduce_fusion
  382.1 4.3 fusion.61
  386.5 75.6 %reduce-scatter.15.cloned.1.call-done = f32[256,1024]{1,0:T(8,128)} async-done(((f32[1024,1024]{1,0:T(8,128)}), f32[256,1024]{1,0:T(8,128)}) %reduce-scatter.15.cloned.1.call-update) | async-done | bytes 1048592 | tf_op jit(solution)/shard_map/reduce_scatter | solution.py:187
  466.5 45.9 %all-gather.17.cloned.1.call-done = bf16[1024,1024]{1,0:T(8,128)(2,1)} async-done(((bf16[256,1024]{1,0:T(8,128)(2,1)}), bf16[1024,1024]{1,0:T(8,128)(2,1)}) %all-gather.17.cloned.1.call-update) | async-done | bytes 2097168 | tf_op jit(solution)/shard_map/all_gather | solution.py:195
  512.4 3.2 convolution_convert_fusion.1
  515.6 2.8 reshape.191
  521.5 19.9 %while.28 = (s32[]{:T(128)}, f32[1024,4,64]{0,2,1:T(8,128)S(1)}, f32[1024,4,64]{0,2,1:T(8,128)S(1)}, bf16[2,512,4,64]{1,3,2,0:T(8,128)(2,1)}, bf16[2,512,4,64]{1...) while((s32[]{:T(128)}, f32[1024,4,64]{0,2,1:T(8,128)S(1)}, ...), condition=%wide.region_17.18_spmd.clone, body=%wide.region_15.17_spmd.clone.sunk | while | flops 1362229248 | bytes 78438664 | solution.py:88
  541.5 3.3 convolution_bitcast_fusion.1
  545.0 3.4 convolution_bitcast_fusion.2
  557.9 6.5 fusion.66
  566.1 5.9 fusion.65
  573.0 3.4 fusion.64
  576.9 40.6 %all-reduce = (f32[1024]{0:T(1024)S(1)}, f32[1024]{0:T(1024)S(1)}, f32[1024]{0:T(1024)}, f32[4096]{0:T(1024)S(1)}, f32[1024]{0:T(1024)}, /*index=5*/f32[1024]{0:...) all-reduce(f32[1024]{0:T(1024)S(1)} %bitcast.165, ...), channel_id=1, replica_groups=mesh['dp'=8,'tensor'=4] {'dp','tensor'}, use_global_device_ids=true, to_apply=%region_26.27 | all-reduce | flops 12288 | bytes 98304 | tf_op jit(solution)/shard_map/psum | solution.py:238
  622.7 36.3 %reduce-scatter.19.cloned.1.call-done = f32[128,256]{0,1:T(8,128)} async-done(((f32[1024,256]{0,1:T(8,128)}), f32[128,256]{0,1:T(8,128)}) %reduce-scatter.19.cloned.1.call-update) | async-done | bytes 131088 | tf_op jit(solution)/shard_map/reduce_scatter | solution.py:225
  660.7 44.1 %reduce-scatter.17.cloned.1.call-done = bf16[256,1024]{1,0:T(8,128)(2,1)} async-done(((bf16[1024,1024]{1,0:T(8,128)(2,1)}), bf16[256,1024]{1,0:T(8,128)(2,1)}) %reduce-scatter.17.cloned.1.call-update) | async-done | bytes 524304 | tf_op jit(solution)/shard_map/reduce_scatter | solution.py:212
  707.0 52.2 %reduce-scatter.29.cloned.1.call-done = f32[1024,128]{1,0:T(8,128)} async-done(((f32[1024,1024]{1,0:T(8,128)}), f32[1024,128]{1,0:T(8,128)}) %reduce-scatter.29.cloned.1.call-update) | async-done | bytes 524304 | tf_op jit(solution)/shard_map/reduce_scatter | solution.py:230
  759.2 55.4 %reduce-scatter.27.cloned.1.call-done = f32[128,1024]{1,0:T(8,128)} async-done(((f32[1024,1024]{1,0:T(8,128)}), f32[128,1024]{1,0:T(8,128)}) %reduce-scatter.27.cloned.1.call-update) | async-done | bytes 524304 | tf_op jit(solution)/shard_map/reduce_scatter | solution.py:229
  814.6 39.8 %reduce-scatter.25.cloned.1.call-done = f32[256,128]{1,0:T(8,128)} async-done(((f32[256,1024]{1,0:T(8,128)}), f32[256,128]{1,0:T(8,128)}) %reduce-scatter.25.cloned.1.call-update) | async-done | bytes 131088 | tf_op jit(solution)/shard_map/reduce_scatter | solution.py:228
  (193 shorter events, 84.3 us)
Async XLA Ops:
  8.0 51.1 %all-gather.7.cloned.1.call-start = ((), (), s32[]{:S(2)}) async-start(), calls=%async_computation.10 | async-start | bytes 2621440 | tf_op jit(solution)/shard_map/all_gather | solution.py:140
  8.8 150.3 %reduce-scatter.11.cloned.1.call-start = ((), (), s32[]{:S(2)}) async-start(), calls=%async_computation.11 | async-start | bytes 5242880 | tf_op jit(solution)/shard_map/reduce_scatter | solution.py:152
  21.7 39.8 %copy-start.16 = (bf16[1024,256]{1,0:T(8,128)(2,1)}, bf16[1024,256]{1,0:T(8,128)(2,1)S(1)}, u32[]{:S(2)}) copy-start(bf16[1024,256]{1,0:T(8,128)(2,1)S(1)} %all_gather.37) | copy-start | bytes 1572868
  59.1 5.4 copy-start.1
  69.0 11.7 %copy-start.18 = (bf16[256,1024]{1,0:T(8,128)(2,1)S(1)}, bf16[256,1024]{1,0:T(8,128)(2,1)}, u32[]{:S(2)}) copy-start(bf16[256,1024]{1,0:T(8,128)(2,1)} %all_gather.40) | copy-start | bytes 1572868
  83.3 75.7 %copy-start.14 = (bf16[256,1024]{1,0:T(8,128)(2,1)S(1)}, bf16[256,1024]{1,0:T(8,128)(2,1)}, u32[]{:S(2)}) copy-start(bf16[256,1024]{1,0:T(8,128)(2,1)} %param.21) | copy-start | bytes 1572868
  83.4 79.2 %copy-start.23 = (bf16[1024]{0:T(1024)(128)(2,1)S(1)}, bf16[1024]{0:T(1024)(128)(2,1)}, u32[]{:S(2)}) copy-start(bf16[1024]{0:T(1024)(128)(2,1)} %param.31) | copy-start | bytes 6148
  83.4 79.3 %all-gather.11.cloned.1.call-start = ((), (), s32[]{:S(2)}) async-start(), calls=%async_computation.13 | async-start | bytes 2359296 | tf_op jit(solution)/shard_map/all_gather | solution.py:136
  84.0 124.0 %all-gather.9.cloned.1.call-start = ((), (), s32[]{:S(2)}) async-start(), calls=%async_computation.12 | async-start | bytes 2621440 | tf_op jit(solution)/shard_map/all_gather | solution.py:159
  161.8 74.9 %all-gather.13.cloned.1.call-start = ((), (), s32[]{:S(2)}) async-start(), calls=%async_computation.14 | async-start | bytes 2359296 | tf_op jit(solution)/shard_map/all_gather | solution.py:137
  162.4 157.8 %reduce-scatter.13.cloned.1.call-start = ((), (), s32[]{:S(2)}) async-start(), calls=%async_computation.15 | async-start | bytes 5242880 | tf_op jit(solution)/shard_map/reduce_scatter | solution.py:163
  243.3 78.8 %copy-start.19 = (bf16[256,1024]{1,0:T(8,128)(2,1)S(1)}, bf16[256,1024]{1,0:T(8,128)(2,1)}, u32[]{:S(2)}) copy-start(bf16[256,1024]{1,0:T(8,128)(2,1)} %param.37) | copy-start | bytes 1572868
  243.3 129.0 %all-gather.15.cloned.1.call-start = ((), (), s32[]{:S(2)}) async-start(), calls=%async_computation.16 | async-start | bytes 2621440 | tf_op jit(solution)/shard_map/all_gather | solution.py:180
  325.8 136.3 %reduce-scatter.15.cloned.1.call-start = ((), (), s32[]{:S(2)}) async-start(), calls=%async_computation.17 | async-start | bytes 5242880 | tf_op jit(solution)/shard_map/reduce_scatter | solution.py:187
  372.3 9.8 %copy-start.28 = (bf16[1024,1024]{1,0:T(8,128)(2,1)S(1)}, bf16[1024,1024]{1,0:T(8,128)(2,1)}, u32[]{:S(2)}) copy-start(bf16[1024,1024]{1,0:T(8,128)(2,1)} %all-gather.11.cloned.1.call-done) | copy-start | bytes 6291460
  386.5 126.0 %all-gather.17.cloned.1.call-start = ((), (), s32[]{:S(2)}) async-start(), calls=%async_computation.18 | async-start | bytes 2621440 | tf_op jit(solution)/shard_map/all_gather | solution.py:195
  466.2 153.1 %reduce-scatter.23.cloned.1.call-start = ((), (), s32[]{:S(2)}) async-start(), calls=%async_computation.22 | async-start | bytes 1179648 | tf_op jit(solution)/shard_map/reduce_scatter | solution.py:227
  522.8 1.8 copy-start.4
  527.2 1.8 copy-start.11
  532.8 1.8 copy-start.4
  544.9 76.2 %reduce-scatter.21.cloned.1.call-start = ((), (), s32[]{:S(2)}) async-start(), calls=%async_computation.21 | async-start | bytes 1179648 | tf_op jit(solution)/shard_map/reduce_scatter | solution.py:226
  545.0 6.0 copy-start.2
  548.5 110.6 %reduce-scatter.19.cloned.1.call-start = ((), (), s32[]{:S(2)}) async-start(), calls=%async_computation.20 | async-start | bytes 1179648 | tf_op jit(solution)/shard_map/reduce_scatter | solution.py:225
  552.7 2.0 copy-start.10
  552.7 2.0 copy-start.17
  552.7 2.8 copy-start.15
  552.7 152.1 %reduce-scatter.17.cloned.1.call-start = ((), (), s32[]{:S(2)}) async-start(), calls=%async_computation.19 | async-start | bytes 2621440 | tf_op jit(solution)/shard_map/reduce_scatter | solution.py:212
  557.6 201.6 %reduce-scatter.29.cloned.1.call-start = ((), (), s32[]{:S(2)}) async-start(), calls=%async_computation.25 | async-start | bytes 4718592 | tf_op jit(solution)/shard_map/reduce_scatter | solution.py:230
  564.5 250.1 %reduce-scatter.27.cloned.1.call-start = ((), (), s32[]{:S(2)}) async-start(), calls=%async_computation.24 | async-start | bytes 4718592 | tf_op jit(solution)/shard_map/reduce_scatter | solution.py:229
  572.0 4.5 copy-start.13
  572.0 132.8 %copy-start.6 = (f32[256,1024]{1,0:T(8,128)S(1)}, f32[256,1024]{1,0:T(8,128)}, u32[]{:S(2)}) copy-start(f32[256,1024]{1,0:T(8,128)} %copy-done.5) | copy-start | bytes 3145732
  572.0 282.3 %reduce-scatter.25.cloned.1.call-start = ((), (), s32[]{:S(2)}) async-start(), calls=%async_computation.23 | async-start | bytes 1179648 | tf_op jit(solution)/shard_map/reduce_scatter | solution.py:228
  (19 other events, 20.6 us)
Sparse Core Ops, SparseCore 0:
  10.4 48.6 all-gather.6
  83.5 75.4 reduce-scatter.10
  325.9 46.3 all-gather.14
  386.6 75.4 reduce-scatter.14
Sparse Core Ops, SparseCore 1:
  85.8 26.4 all-gather.10
  161.9 46.0 all-gather.8
  209.9 26.8 all-gather.12
  243.4 76.7 reduce-scatter.12
  466.3 46.0 all-gather.16
  544.9 34.7 reduce-scatter.22
  583.1 35.9 reduce-scatter.20
  623.0 36.0 reduce-scatter.18
  661.3 43.5 reduce-scatter.16
  708.8 50.4 reduce-scatter.28
  763.4 51.1 reduce-scatter.26
  818.4 35.9 reduce-scatter.24
where the time goes:
time: 870 us; the launch traced here: 862 us
  waiting for transfers between devices  613 us (70%)
  matrix products  98.7 us (11%)
  blocking collectives  84.6 us (10%)
  local copies, waits for them, and re-layouts  25.2 us (3%)
  other arithmetic  22.5 us (3%)
  between operations  16.3 us (2%)
    reduce_scatter x1, waiting for transfers between devices, body(): lax.psum_scatter(product(hidden, shrink_full), 'tensor', scatter_dimensio...  76.2 us
    reduce_scatter x1, waiting for transfers between devices, body(): lax.psum_scatter(product_last(expanded_low, expand_back), 'tensor', scatt...  75.6 us
    reduce_scatter x1, waiting for transfers between devices, body(): lax.psum_scatter(product(mixture, mixing_full), 'tensor', scatter_dimensi...  74.9 us
    reduce_scatter x1, waiting for transfers between devices, body(): lax.psum_scatter(expand_local, 'dp', scatter_dimension=0, tiled=True)  55.4 us
    reduce_scatter x1, waiting for transfers between devices, body(): lax.psum_scatter(shrink_local, 'dp', scatter_dimension=1, tiled=True)  52.2 us
    all_gather x1, waiting for transfers between devices, body(): lax.all_gather(summed_grad.astype(jnp.bfloat16), 'tensor', axis=0, tiled=...  46.5 us
    all_gather x1, waiting for transfers between devices, body(): lax.all_gather(attended_grad.astype(jnp.bfloat16), 'tensor', axis=0, tile...  45.9 us
    all_gather x1, waiting for transfers between devices, body(): lax.all_gather(first_norm.astype(jnp.bfloat16), 'tensor', axis=0, tiled=T...  45.3 us
  transfers between devices with their start and end apart: 16, of which 13 were waited for; matrix products, arithmetic and copies ran while one was open for 6% of the time, Pallas kernels for 0%

commit v1 on v0

--- a/solution.py
+++ b/solution.py
@@ -150,7 +150,7 @@
         block_rows,
     )
     attended_part = lax.psum_scatter(
-        product(mixture, mixing_full), "tensor", scatter_dimension=0, tiled=True
+        product(mixture, mixing_full).astype(jnp.bfloat16), "tensor", scatter_dimension=0, tiled=True
     )
     attended = layer_input.astype(jnp.float32) + attended_part + mixing_offset.astype(jnp.float32)
     first_norm, first_back = jax.vjp(
@@ -161,22 +161,14 @@
     hidden_act, gelu_back = jax.vjp(gelu_exact, expanded)
     hidden = hidden_act.astype(jnp.bfloat16)
     shrunk = lax.psum_scatter(
-        product(hidden, shrink_full), "tensor", scatter_dimension=0, tiled=True
+        product(hidden, shrink_full).astype(jnp.bfloat16), "tensor", scatter_dimension=0, tiled=True
     )
     summed = first_norm + shrunk + shrink_offset.astype(jnp.float32)
     normalized, second_back = jax.vjp(
         layer_norm, summed, second_gain.astype(jnp.float32), second_shift.astype(jnp.float32)
     )
     summed_grad, gain_second, shift_second = second_back(cotangent.astype(jnp.float32))
-    regathered = (
-        lax.all_gather(query_weight, "dp", axis=0, tiled=True),
-        lax.all_gather(key_weight, "dp", axis=0, tiled=True),
-        lax.all_gather(value_weight, "dp", axis=0, tiled=True),
-        lax.all_gather(mixing_weight, "dp", axis=1, tiled=True),
-        lax.all_gather(expand_weight, "dp", axis=0, tiled=True),
-        lax.all_gather(shrink_weight, "dp", axis=1, tiled=True),
-    )
-    query_back, key_back, value_back, mixing_back, expand_back, shrink_back = regathered
+    query_back, key_back, value_back, mixing_back, expand_back, shrink_back = gathered
     branch_rows = lax.all_gather(summed_grad.astype(jnp.bfloat16), "tensor", axis=0, tiled=True)
     shrink_local = product_rows(hidden, branch_rows)
     hidden_grad = product_last(branch_rows, shrink_back)
@@ -185,7 +177,7 @@
     expand_local = product_rows(normed, expanded_low)
     first_grad = (
         lax.psum_scatter(
-            product_last(expanded_low, expand_back), "tensor", scatter_dimension=0, tiled=True
+            product_last(expanded_low, expand_back).astype(jnp.bfloat16), "tensor", scatter_dimension=0, tiled=True
         )
         + summed_grad
     )
@@ -222,12 +214,12 @@
         + attended_grad
     )
     query_grad, key_grad, value_grad, mixing_grad, expand_grad, shrink_grad = (
-        lax.psum_scatter(query_local, "dp", scatter_dimension=0, tiled=True),
-        lax.psum_scatter(key_local, "dp", scatter_dimension=0, tiled=True),
-        lax.psum_scatter(value_local, "dp", scatter_dimension=0, tiled=True),
-        lax.psum_scatter(mixing_local, "dp", scatter_dimension=1, tiled=True),
-        lax.psum_scatter(expand_local, "dp", scatter_dimension=0, tiled=True),
-        lax.psum_scatter(shrink_local, "dp", scatter_dimension=1, tiled=True),
+        lax.psum_scatter(query_local.astype(jnp.bfloat16), "dp", scatter_dimension=0, tiled=True).astype(jnp.float32),
+        lax.psum_scatter(key_local.astype(jnp.bfloat16), "dp", scatter_dimension=0, tiled=True).astype(jnp.float32),
+        lax.psum_scatter(value_local.astype(jnp.bfloat16), "dp", scatter_dimension=0, tiled=True).astype(jnp.float32),
+        lax.psum_scatter(mixing_local.astype(jnp.bfloat16), "dp", scatter_dimension=1, tiled=True).astype(jnp.float32),
+        lax.psum_scatter(expand_local.astype(jnp.bfloat16), "dp", scatter_dimension=0, tiled=True).astype(jnp.float32),
+        lax.psum_scatter(shrink_local.astype(jnp.bfloat16), "dp", scatter_dimension=1, tiled=True).astype(jnp.float32),
     )
     tensor_index = lax.axis_index("tensor")
     selector = (jnp.arange(tensor_size)[:, None] == tensor_index).astype(jnp.float32)

time: 870 us -> 714 us (0.82)
  waiting for transfers between devices: 613 us -> 446 us
    reduce_scatter x9 -> x4, waiting for transfers between devices: 410 us -> 159 us  [the longest x1 43.9 us: body(): lax.psum_scatter(product(hidden, shrink_full).astype(jnp.bfloat16), 'tens...]
    unnamed x16 -> x21, waiting for transfers between devices: 1.94 us -> 101 us
    all_gather x1, waiting for transfers between devices: 45.9 us -> 31.3 us  [body(): lax.all_gather(attended_grad.astype(jnp.bfloat16), 'tensor', axis=0, tile...]
    unnamed x59 -> x71, local copies, waits for them, and re-layouts: 14.4 us -> 21.5 us
  transfers between devices with their start and end apart: 16 -> 16, of which waited for: 13 -> 13; matrix products, arithmetic and copies ran while one was open for 6% -> 14% of each run, Pallas kernels for 0% -> 0%
where the time goes in v1:
time: 714 us; the launch traced here: 704 us
  waiting for transfers between devices  446 us (62%)
  matrix products  99.2 us (14%)
  blocking collectives  81.9 us (11%)
  local copies, waits for them, and re-layouts  30.4 us (4%)
  other arithmetic  29.1 us (4%)
  between operations  16.2 us (2%)
    unnamed x21, waiting for transfers between devices  101 us
    all_gather x1, waiting for transfers between devices, body(): lax.all_gather(summed_grad.astype(jnp.bfloat16), 'tensor', axis=0, tiled=...  44.5 us
    reduce_scatter x1, waiting for transfers between devices, body(): lax.psum_scatter((product_last(query_low, query_back) * scaling + product...  44.2 us
    all_gather x1, waiting for transfers between devices, body(): lax.all_gather(first_norm.astype(jnp.bfloat16), 'tensor', axis=0, tiled=T...  44.1 us
    reduce_scatter x1, waiting for transfers between devices, body(): lax.psum_scatter(product(hidden, shrink_full).astype(jnp.bfloat16), 'tens...  43.9 us
    reduce_scatter x1, waiting for transfers between devices, body(): lax.psum_scatter(product_last(expanded_low, expand_back).astype(jnp.bfloa...  42.8 us
    reduce_scatter x1, waiting for transfers between devices, body(): lax.psum_scatter(product(mixture, mixing_full).astype(jnp.bfloat16), 'ten...  42 us
    psum x1, blocking collectives, body(): lax.psum((gain_first, shift_first, gain_second, shift_second, mixing_sum,...  40.7 us
  transfers between devices with their start and end apart: 16, of which 13 were waited for; matrix products, arithmetic and copies ran while one was open for 14% of the time, Pallas kernels for 0%

profile of v1, /device:TPU:0, one launch (start us, length us, event | category | flops | bytes accessed | tf_op | source)
XLA Modules:
  0.0 704.4 jit_solution(7860083018517622834)
XLA Ops:
  10.1 11.6 %all_gather.31 = bf16[1024,256]{1,0:T(8,128)(2,1)S(1)} all-gather(bf16[128,256]{1,0:T(8,128)(2,1)} %param.22), channel_id=1, replica_groups=mesh['dp'=8,'tensor'=4] {'dp'}, dimensions={0}, use_global_device_ids=true | all-gather | bytes 589824 | tf_op jit(solution)/shard_map/all_gather | solution.py:132
  21.7 9.5 %all_gather.32 = bf16[1024,256]{1,0:T(8,128)(2,1)S(1)} all-gather(bf16[128,256]{1,0:T(8,128)(2,1)} %param.23), channel_id=1, replica_groups=mesh['dp'=8,'tensor'=4] {'dp'}, dimensions={0}, use_global_device_ids=true | all-gather | bytes 589824 | tf_op jit(solution)/shard_map/all_gather | solution.py:133
  31.3 9.2 %all_gather.33 = bf16[1024,256]{1,0:T(8,128)(2,1)S(1)} all-gather(bf16[128,256]{1,0:T(8,128)(2,1)} %param.24), channel_id=1, replica_groups=mesh['dp'=8,'tensor'=4] {'dp'}, dimensions={0}, use_global_device_ids=true | all-gather | bytes 589824 | tf_op jit(solution)/shard_map/all_gather | solution.py:134
  40.4 10.9 %all_gather.34 = bf16[256,1024]{1,0:T(8,128)(2,1)} all-gather(bf16[256,128]{1,0:T(8,128)(2,1)} %param.25), channel_id=1, replica_groups=mesh['dp'=8,'tensor'=4] {'dp'}, dimensions={1}, use_global_device_ids=true | all-gather | bytes 589824 | tf_op jit(solution)/shard_map/all_gather | solution.py:135
  51.3 7.8 %all-gather.7.cloned.1.call-done = bf16[1024,1024]{1,0:T(8,128)(2,1)} async-done(((bf16[256,1024]{1,0:T(8,128)(2,1)}), bf16[1024,1024]{1,0:T(8,128)(2,1)}) %all-gather.7.cloned.1.call-update) | async-done | bytes 2097168 | tf_op jit(solution)/shard_map/all_gather | solution.py:140
  64.8 3.1 fusion.44
  68.0 12.4 %while.27 = (s32[]{:T(128)}, bf16[2,512,4,64]{1,3,2,0:T(8,128)(2,1)S(1)}, f32[2,4,512]{2,1,0:T(4,128)S(1)}, bf16[2,512,4,64]{1,3,2,0:T(8,128)(2,1)S(1)}, bf16[10...) while((s32[]{:T(128)}, bf16[2,512,4,64]{1,3,2,0:T(8,128)(2,1)S(1)}, ...), condition=%wide.region_3.4_spmd, body=%wide.region_0.3_spmd.sunk | while | flops 549582848 | bytes 26804320 | solution.py:52
  71.2 3.0 fusion.131
  83.9 42.0 %reduce-scatter.21.cloned.1.call-done = bf16[256,1024]{1,0:T(8,128)(2,1)} async-done(((bf16[1024,1024]{1,0:T(8,128)(2,1)}), bf16[256,1024]{1,0:T(8,128)(2,1)}) %reduce-scatter.21.cloned.1.call-update) | async-done | bytes 524304 | tf_op jit(solution)/shard_map/reduce_scatter | solution.py:152
  131.7 44.1 %all-gather.9.cloned.1.call-done = bf16[1024,1024]{1,0:T(8,128)(2,1)} async-done(((bf16[256,1024]{1,0:T(8,128)(2,1)}), bf16[1024,1024]{1,0:T(8,128)(2,1)}) %all-gather.9.cloned.1.call-update) | async-done | bytes 2097168 | tf_op jit(solution)/shard_map/all_gather | solution.py:159
  175.8 14.9 %multiply_convert_fusion.1 = (bf16[1024,1024]{1,0:T(8,128)(2,1)}, f32[1024,1024]{1,0:T(8,128)}, f32[1024,1024]{1,0:T(8,128)}) fusion(f32[1024]{0:T(1024)S(1)} %convert_element_type.190, bf16[1024,1024]{1,0:T(8,128)(2,1)} %all-gather.9.cloned.1.call-done, bf16[1024,1024]{1,0:T(8,128)(2,1)} %all-gather.11.cloned.1.call-done), kind=kOutput, calls=%fused_computation.45 | convolution fusion | flops 2216689664 | bytes 14684160 | tf_op jit(solution)/shard_map/dot_general | solution.py:21
  190.7 13.9 %all-gather.13.cloned.1.call-done = bf16[1024,1024]{1,0:T(8,128)(2,1)} async-done(((bf16[1024,128]{1,0:T(8,128)(2,1)}), bf16[1024,1024]{1,0:T(8,128)(2,1)}) %all-gather.13.cloned.1.call-update) | async-done | bytes 2097168 | tf_op jit(solution)/shard_map/all_gather | solution.py:137
  204.5 6.0 convolution_convert_fusion.4
  210.6 43.9 %reduce-scatter.23.cloned.1.call-done = bf16[256,1024]{1,0:T(8,128)(2,1)} async-done(((bf16[1024,1024]{1,0:T(8,128)(2,1)}), bf16[256,1024]{1,0:T(8,128)(2,1)}) %reduce-scatter.23.cloned.1.call-update) | async-done | bytes 524304 | tf_op jit(solution)/shard_map/reduce_scatter | solution.py:163
  260.6 44.5 %all-gather.15.cloned.1.call-done = bf16[1024,1024]{1,0:T(8,128)(2,1)} async-done(((bf16[256,1024]{1,0:T(8,128)(2,1)}), bf16[1024,1024]{1,0:T(8,128)(2,1)}) %all-gather.15.cloned.1.call-update) | async-done | bytes 2097168 | tf_op jit(solution)/shard_map/all_gather | solution.py:172
  305.1 8.5 %convert_reduce_fusion = (f32[1024]{0:T(1024)S(1)}, bf16[1024,1024]{1,0:T(8,128)(2,1)S(1)}) fusion(f32[1024,1024]{1,0:T(8,128)} %get-tuple-element.287, f32[1024,1024]{1,0:T(8,128)} %get-tuple-element.297, f32[1024]{0:T(1024)S(1)} %convert_element_type.190, bf16[1024,1024]{1,0:T(8,128)(2,1)} %all-gather.15.cloned.1.call-done, ...), kind=kOutput, calls=%fused_computation.42 | convolution fusion | flops 2165308416 | bytes 14688256 | tf_op jit(solution)/shard_map/dot_general | solution.py:29
  315.0 3.7 convolution_convert_fusion.3
  318.7 42.8 %reduce-scatter.25.cloned.1.call-done = bf16[256,1024]{1,0:T(8,128)(2,1)} async-done(((bf16[1024,1024]{1,0:T(8,128)(2,1)}), bf16[256,1024]{1,0:T(8,128)(2,1)}) %reduce-scatter.25.cloned.1.call-update) | async-done | bytes 524304 | tf_op jit(solution)/shard_map/reduce_scatter | solution.py:179
  367.0 4.6 convolution_convert_fusion.1
  374.2 6.1 convolution_convert_fusion.2
  380.6 31.3 %all-gather.17.cloned.1.call-done = bf16[1024,1024]{1,0:T(8,128)(2,1)} async-done(((bf16[256,1024]{1,0:T(8,128)(2,1)}), bf16[1024,1024]{1,0:T(8,128)(2,1)}) %all-gather.17.cloned.1.call-update) | async-done | bytes 2097168 | tf_op jit(solution)/shard_map/all_gather | solution.py:187
  411.9 3.3 convolution_convert_fusion.6
  417.2 3.2 convolution_convert_fusion.9
  426.4 21.4 %while.28 = (s32[]{:T(128)}, f32[1024,4,64]{0,2,1:T(8,128)S(1)}, f32[1024,4,64]{0,2,1:T(8,128)S(1)}, bf16[2,512,4,64]{1,3,2,0:T(8,128)(2,1)}, bf16[2,512,4,64]{1...) while((s32[]{:T(128)}, f32[1024,4,64]{0,2,1:T(8,128)S(1)}, ...), condition=%wide.region_17.18_spmd.clone, body=%wide.region_15.17_spmd.clone.sunk | while | flops 1362229248 | bytes 76341480 | solution.py:88
  429.6 3.3 multiply_reduce_fusion.6
  440.3 3.3 multiply_reduce_fusion.6
  469.8 30.0 %reduce-scatter.29.cloned.1.call-done = bf16[128,1024]{1,0:T(8,128)(2,1)} async-done(((bf16[1024,1024]{1,0:T(8,128)(2,1)}), bf16[128,1024]{1,0:T(8,128)(2,1)}) %reduce-scatter.29.cloned.1.call-update) | async-done | bytes 262160 | tf_op jit(solution)/shard_map/reduce_scatter | solution.py:221
  502.0 40.7 %all-reduce = (f32[1024]{0:T(1024)S(1)}, f32[1024]{0:T(1024)S(1)}, f32[1024]{0:T(1024)}, f32[4096]{0:T(1024)S(1)}, f32[1024]{0:T(1024)}, /*index=5*/f32[1024]{0:...) all-reduce(f32[1024]{0:T(1024)S(1)} %bitcast.175, ...), channel_id=1, replica_groups=mesh['dp'=8,'tensor'=4] {'dp','tensor'}, use_global_device_ids=true, to_apply=%region_26.27 | all-reduce | flops 12288 | bytes 98304 | tf_op jit(solution)/shard_map/psum | solution.py:230
  546.2 28.1 %reduce-scatter.31.cloned.1.call-done = bf16[128,256]{1,0:T(8,128)(2,1)} async-done(((bf16[1024,256]{1,0:T(8,128)(2,1)}), bf16[128,256]{1,0:T(8,128)(2,1)}) %reduce-scatter.31.cloned.1.call-update) | async-done | bytes 65552
  576.0 35.8 %reduce-scatter.33.cloned.1.call-done = bf16[128,256]{1,0:T(8,128)(2,1)} async-done(((bf16[1024,256]{1,0:T(8,128)(2,1)}), bf16[128,256]{1,0:T(8,128)(2,1)}) %reduce-scatter.33.cloned.1.call-update) | async-done | bytes 65552
  613.6 35.3 %reduce-scatter.35.cloned.1.call-done = bf16[128,256]{1,0:T(8,128)(2,1)} async-done(((bf16[1024,256]{1,0:T(8,128)(2,1)}), bf16[128,256]{1,0:T(8,128)(2,1)}) %reduce-scatter.35.cloned.1.call-update) | async-done | bytes 65552
  650.6 44.2 %reduce-scatter.27.cloned.1.call-done = bf16[256,1024]{1,0:T(8,128)(2,1)} async-done(((bf16[1024,1024]{1,0:T(8,128)(2,1)}), bf16[256,1024]{1,0:T(8,128)(2,1)}) %reduce-scatter.27.cloned.1.call-update) | async-done | bytes 524304 | tf_op jit(solution)/shard_map/reduce_scatter | solution.py:204
  (200 shorter events, 99.3 us)
Async XLA Ops:
  8.0 51.1 %all-gather.7.cloned.1.call-start = ((), (), s32[]{:S(2)}) async-start(), calls=%async_computation.10 | async-start | bytes 2621440 | tf_op jit(solution)/shard_map/all_gather | solution.py:140
  8.8 117.1 %reduce-scatter.21.cloned.1.call-start = ((), (), s32[]{:S(2)}) async-start(), calls=%async_computation.11 | async-start | bytes 2621440 | tf_op jit(solution)/shard_map/reduce_scatter | solution.py:152
  21.7 39.7 %copy-start.11 = (bf16[1024,256]{1,0:T(8,128)(2,1)}, bf16[1024,256]{1,0:T(8,128)(2,1)S(1)}, u32[]{:S(2)}) copy-start(bf16[1024,256]{1,0:T(8,128)(2,1)S(1)} %all_gather.31) | copy-start | bytes 1572868
  31.2 31.2 %copy-start.13 = (bf16[1024,256]{1,0:T(8,128)(2,1)}, bf16[1024,256]{1,0:T(8,128)(2,1)S(1)}, u32[]{:S(2)}) copy-start(bf16[1024,256]{1,0:T(8,128)(2,1)S(1)} %all_gather.32) | copy-start | bytes 1572868
  40.4 24.4 %copy-start.9 = (bf16[1024,256]{1,0:T(8,128)(2,1)}, bf16[1024,256]{1,0:T(8,128)(2,1)S(1)}, u32[]{:S(2)}) copy-start(bf16[1024,256]{1,0:T(8,128)(2,1)S(1)} %all_gather.33) | copy-start | bytes 1572868
  68.0 13.1 %copy-start.18 = (bf16[256,1024]{1,0:T(8,128)(2,1)S(1)}, bf16[256,1024]{1,0:T(8,128)(2,1)}, u32[]{:S(2)}) copy-start(bf16[256,1024]{1,0:T(8,128)(2,1)} %all_gather.34) | copy-start | bytes 1572868
  80.4 45.5 %copy-start = (bf16[256,1024]{1,0:T(8,128)(2,1)S(1)}, bf16[256,1024]{1,0:T(8,128)(2,1)}, u32[]{:S(2)}) copy-start(bf16[256,1024]{1,0:T(8,128)(2,1)} %param.21) | copy-start | bytes 1572868
  81.1 49.6 %copy-start.19 = (bf16[32,8,2,512]{3,1,2,0:T(8,128)(2,1)}, bf16[32,8,2,512]{3,1,2,0:T(8,128)(2,1)S(1)}, u32[]{:S(2)}) copy-start(bf16[32,8,2,512]{3,1,2,0:T(8,128)(2,1)S(1)} %copy.74) | copy-start | bytes 1572868
  83.1 48.4 %copy-start.23 = (bf16[1024]{0:T(1024)(128)(2,1)S(1)}, bf16[1024]{0:T(1024)(128)(2,1)}, u32[]{:S(2)}) copy-start(bf16[1024]{0:T(1024)(128)(2,1)} %param.31) | copy-start | bytes 6148
  83.2 48.5 %all-gather.11.cloned.1.call-start = ((), (), s32[]{:S(2)}) async-start(), calls=%async_computation.13 | async-start | bytes 2359296 | tf_op jit(solution)/shard_map/all_gather | solution.py:136
  83.8 92.0 %all-gather.9.cloned.1.call-start = ((), (), s32[]{:S(2)}) async-start(), calls=%async_computation.12 | async-start | bytes 2621440 | tf_op jit(solution)/shard_map/all_gather | solution.py:159
  130.8 73.8 %all-gather.13.cloned.1.call-start = ((), (), s32[]{:S(2)}) async-start(), calls=%async_computation.14 | async-start | bytes 2359296 | tf_op jit(solution)/shard_map/all_gather | solution.py:137
  131.3 123.2 %reduce-scatter.23.cloned.1.call-start = ((), (), s32[]{:S(2)}) async-start(), calls=%async_computation.15 | async-start | bytes 2621440 | tf_op jit(solution)/shard_map/reduce_scatter | solution.py:163
  204.5 6.1 copy-start.24
  204.5 6.1 copy-start.25
  204.5 6.1 copy-start.26
  204.5 50.0 %copy-start.2 = (bf16[256,1024]{1,0:T(8,128)(2,1)S(1)}, bf16[256,1024]{1,0:T(8,128)(2,1)}, u32[]{:S(2)}) copy-start(bf16[256,1024]{1,0:T(8,128)(2,1)} %reduce-scatter.21.cloned.1.call-done) | copy-start | bytes 1572868
  210.5 45.9 %copy-start.17 = (bf16[256,1024]{1,0:T(8,128)(2,1)S(1)}, bf16[256,1024]{1,0:T(8,128)(2,1)}, u32[]{:S(2)}) copy-start(bf16[256,1024]{1,0:T(8,128)(2,1)} %param.37) | copy-start | bytes 1572868
  210.5 94.6 %all-gather.15.cloned.1.call-start = ((), (), s32[]{:S(2)}) async-start(), calls=%async_computation.16 | async-start | bytes 2621440 | tf_op jit(solution)/shard_map/all_gather | solution.py:172
  260.1 101.4 %reduce-scatter.25.cloned.1.call-start = ((), (), s32[]{:S(2)}) async-start(), calls=%async_computation.17 | async-start | bytes 2621440 | tf_op jit(solution)/shard_map/reduce_scatter | solution.py:179
  305.1 9.8 %copy-start.27 = (bf16[1024,1024]{1,0:T(8,128)(2,1)S(1)}, bf16[1024,1024]{1,0:T(8,128)(2,1)}, u32[]{:S(2)}) copy-start(bf16[1024,1024]{1,0:T(8,128)(2,1)} %all-gather.11.cloned.1.call-done) | copy-start | bytes 6291460
  318.7 93.2 %all-gather.17.cloned.1.call-start = ((), (), s32[]{:S(2)}) async-start(), calls=%async_computation.18 | async-start | bytes 2621440 | tf_op jit(solution)/shard_map/all_gather | solution.py:187
  366.9 100.8 %reduce-scatter.39.cloned.1.call-start = ((), (), s32[]{:S(2)}) async-start(), calls=%async_computation.25 | async-start | bytes 2359296
  374.2 125.6 %reduce-scatter.29.cloned.1.call-start = ((), (), s32[]{:S(2)}) async-start(), calls=%async_computation.20 | async-start | bytes 2359296 | tf_op jit(solution)/shard_map/reduce_scatter | solution.py:221
  380.3 164.2 %reduce-scatter.37.cloned.1.call-start = ((), (), s32[]{:S(2)}) async-start(), calls=%async_computation.24 | async-start | bytes 589824
  425.6 148.8 %reduce-scatter.31.cloned.1.call-start = ((), (), s32[]{:S(2)}) async-start(), calls=%async_computation.21 | async-start | bytes 589824
  453.0 158.8 %reduce-scatter.33.cloned.1.call-start = ((), (), s32[]{:S(2)}) async-start(), calls=%async_computation.22 | async-start | bytes 589824
  455.5 4.6 copy-start.14
  456.5 192.4 %reduce-scatter.35.cloned.1.call-start = ((), (), s32[]{:S(2)}) async-start(), calls=%async_computation.23 | async-start | bytes 589824
  462.8 232.0 %reduce-scatter.27.cloned.1.call-start = ((), (), s32[]{:S(2)}) async-start(), calls=%async_computation.19 | async-start | bytes 2621440 | tf_op jit(solution)/shard_map/reduce_scatter | solution.py:204
  467.6 34.0 %copy-start.8 = (bf16[2,512,4,64]{1,3,2,0:T(8,128)(2,1)S(1)}, bf16[2,512,4,64]{1,3,2,0:T(8,128)(2,1)}, u32[]{:S(2)}) copy-start(bf16[2,512,4,64]{1,3,2,0:T(8,128)(2,1)} %get-tuple-element.101) | copy-start | bytes 1572868
  467.6 227.3 %copy-start.5 = (f32[256,1024]{1,0:T(8,128)S(1)}, f32[256,1024]{1,0:T(8,128)}, u32[]{:S(2)}) copy-start(f32[256,1024]{1,0:T(8,128)} %copy-done.4) | copy-start | bytes 3145732
  (16 other events, 38.6 us)
Sparse Core Ops, SparseCore 0:
  10.4 48.6 all-gather.6
  83.3 42.5 reduce-scatter.20
  210.6 43.8 reduce-scatter.22
  318.8 42.6 reduce-scatter.24
Sparse Core Ops, SparseCore 1:
  85.7 26.4 all-gather.10
  130.8 44.9 all-gather.8
  177.7 26.8 all-gather.12
  260.2 44.8 all-gather.14
  367.0 44.8 all-gather.16
  415.6 39.9 reduce-scatter.38
  458.6 41.1 reduce-scatter.28
  503.0 34.1 reduce-scatter.36
  540.1 34.1 reduce-scatter.30
  577.7 34.1 reduce-scatter.32
  614.8 34.1 reduce-scatter.34
  651.3 43.5 reduce-scatter.26

commit v2 on v1

v2 whole, which is shorter than its diff:
```python
import functools

import jax
import jax.numpy as jnp
from jax import lax
from jax.experimental import pallas as pl
from jax.experimental.pallas import tpu as pltpu
from jax.sharding import PartitionSpec as P

HD = 64
EPSILON = 1e-05
MESH = pl.DeviceIdType.MESH
BF = jnp.bfloat16
F32 = jnp.float32
NN = (((1,), (0,)), ((), ()))
NT = (((1,), (1,)), ((), ()))
TN = (((0,), (0,)), ((), ()))
VMEM_LIMIT = 60 * 1024 * 1024
TILE = 512


def mm(left, right, dims):
    return lax.dot_general(left, right, dims, preferred_element_type=F32)


def layer_norm(inputs, gain, shift):
    centered = inputs - jnp.mean(inputs, axis=-1, keepdims=True)
    variance = jnp.mean(centered * centered, axis=-1, keepdims=True)
    return centered * lax.rsqrt(variance + EPSILON) * gain + shift


def norm_parts(inputs):
    centered = inputs - jnp.mean(inputs, axis=-1, keepdims=True)
    variance = jnp.mean(centered * centered, axis=-1, keepdims=True)
    rate = lax.rsqrt(variance + EPSILON)
    return centered * rate, rate


def norm_back(upstream, gain, normal, rate):
    scaled = upstream * gain
    mean_scaled = jnp.mean(scaled, axis=-1, keepdims=True)
    mean_normal = jnp.mean(scaled * normal, axis=-1, keepdims=True)
    return rate * (scaled - mean_scaled - normal * mean_normal)


def column_sum(block):
    return jnp.sum(block, axis=0, keepdims=True)


def tiles(width, body):
    step = min(TILE, width)

    def one(index, carry):
        body(pl.ds(pl.multiple_of(index * step, step), step))
        return carry

    lax.fori_loop(0, width // step, one, 0)


def feed_kernel(
    chunks,
    attended_ref,
    cotangent_ref,
    expand_ref,
    shrink_ref,
    expand_offset_ref,
    vectors_ref,
    output_ref,
    attended_grad_ref,
    expand_grad_ref,
    shrink_grad_ref,
    expand_sum_ref,
    sums_ref,
    normed,
    hidden,
    slope,
    expanded_low,
    summed_low,
    own_part,
    summed_grad,
    send_part,
    recv_part,
    send_sem,
    recv_sem,
):
    rows, width = attended_ref.shape
    slices, _, units = expand_ref.shape
    step = rows // chunks
    t = lax.axis_index("tensor")
    partner = {"tensor": t ^ 1}
    first_gain = vectors_ref[0:1, :]
    first_shift = vectors_ref[1:2, :]
    second_gain = vectors_ref[2:3, :]
    second_shift = vectors_ref[3:4, :]
    shrink_offset = vectors_ref[4:5, :]

    def exchange(kind, chunk, source, target):
        return pltpu.make_async_remote_copy(
            src_ref=source,
            dst_ref=target,
            send_sem=send_sem.at[kind, chunk],
            recv_sem=recv_sem.at[kind, chunk],
            device_id=partner,
            device_id_type=MESH,
        )

    def own(chunk):
        return pl.ds(chunk * step, step)

    def other(chunk):
        return pl.ds(rows + chunk * step, step)

    copies = [
        [exchange(0, c, normed.at[own(c)], normed.at[other(c)]) for c in range(chunks)],
        [
            exchange(1, c, send_part.at[0, own(c)], recv_part.at[0, own(c)])
            for c in range(chunks)
        ],
        [exchange(2, c, summed_low.at[own(c)], summed_low.at[other(c)]) for c in range(chunks)],
        [
            exchange(3, c, send_part.at[1, own(c)], recv_part.at[1, own(c)])
            for c in range(chunks)
        ],
    ]

    barrier = pltpu.get_barrier_semaphore()
    pl.semaphore_signal(barrier, inc=1, device_id=partner, device_id_type=MESH)
    for c in range(chunks):
        normal, _ = norm_parts(attended_ref[own(c), :])
        normed[own(c), :] = (normal * first_gain + first_shift).astype(BF)
    pl.semaphore_wait(barrier, 1)
    for c in range(chunks):
        copies[0][c].start()

    def forward(place, store):
        for s in range(slices):

            def grow(tile):
                value = mm(normed[place, :], expand_ref[s, :, tile], NN)
                value = value + expand_offset_ref[s, :, tile]
                share = 0.5 * (1.0 + lax.erf(value * 0.7071067811865476))
                density = jnp.exp(-0.5 * value * value) * 0.3989422804014327
                hidden[s, place, tile] = (value * share).astype(BF)
                slope[s, place, tile] = (share + value * density).astype(BF)

            tiles(units, grow)

        def shrink(tile):
            total = mm(hidden[0, place, :], shrink_ref[0, tile, :], NT)
            for s in range(1, slices):
                total = total + mm(hidden[s, place, :], shrink_ref[s, tile, :], NT)
            store(tile, total)

        tiles(width, shrink)

    def backward(place, store):
        for s in range(slices):

            def narrow(tile):
                value = mm(summed_low[place, :], shrink_ref[s, :, tile], NN)
                value = value * slope[s, place, tile].astype(F32)
                expanded_low[s, place, tile] = value.astype(BF)

            tiles(units, narrow)

        def widen(tile):
            total = mm(expanded_low[0, place, :], expand_ref[0, tile, :], NT)
            for s in range(1, slices):
                total = total + mm(expanded_low[s, place, :], expand_ref[s, tile, :], NT)
            store(tile, total)

        tiles(width, widen)

    def keep(tile, total):
        own_part[:, tile] = total

    def pass_on(which, chunk):
        def store(tile, total):
            send_part[which, own(chunk), tile] = total.astype(BF)

        return store

    forward(pl.ds(0, rows), keep)
    for c in range(chunks):
        copies[0][c].wait_recv()
        forward(other(c), pass_on(0, c))
        copies[1][c].start()

    sums_ref[...] = jnp.zeros_like(sums_ref)
    for c in range(chunks):
        copies[1][c].wait_recv()
        normal, _ = norm_parts(attended_ref[own(c), :])
        first_norm = normal * first_gain + first_shift
        summed = (
            first_norm
            + (own_part[own(c), :] + recv_part[0, own(c), :].astype(F32))
            + shrink_offset
        )
        normal, rate = norm_parts(summed)
        output_ref[own(c), :] = (normal * second_gain + second_shift).astype(BF)
        upstream = cotangent_ref[own(c), :].astype(F32)
        grad = norm_back(upstream, second_gain, normal, rate)
        summed_grad[own(c), :] = grad
        summed_low[own(c), :] = grad.astype(BF)
        copies[2][c].start()
        sums_ref[0:1, :] += column_sum(upstream * normal)
        sums_ref[1:2, :] += column_sum(upstream)
        sums_ref[2:3, :] += column_sum(grad)

    backward(pl.ds(0, rows), keep)
    for c in range(chunks):
        copies[2][c].wait_recv()
        backward(other(c), pass_on(1, c))
        copies[3][c].start()

    for s in range(slices):

        def weigh(tile):
            left = min(TILE, width)
            for m in range(width // left):
                part = pl.ds(m * left, left)
                shrink_grad_ref[s, part, tile] = mm(
                    summed_low[:, part], hidden[s, :, tile], TN
                ).astype(BF)
                expand_grad_ref[s, part, tile] = mm(
                    normed[:, part], expanded_low[s, :, tile], TN
                ).astype(BF)
            expand_sum_ref[s, :, tile] = column_sum(expanded_low[s, :, tile].astype(F32))

        tiles(units, weigh)

    for c in range(chunks):
        copies[3][c].wait_recv()
        normal, rate = norm_parts(attended_ref[own(c), :])
        upstream = summed_grad[own(c), :] + (
            own_part[own(c), :] + recv_part[1, own(c), :].astype(F32)
        )
        grad = norm_back(upstream, first_gain, normal, rate)
        attended_grad_ref[own(c), :] = grad
        sums_ref[3:4, :] += column_sum(upstream * normal)
        sums_ref[4:5, :] += column_sum(upstream)
        sums_ref[5:6, :] += column_sum(grad)
    for kind in range(4):
        for c in range(chunks):
            copies[kind][c].wait_send()


def feed_forward(attended, cotangent, expand, shrink, expand_offset, vectors):
    rows, width = attended.shape
    slices, _, units = expand.shape
    chunks = 2
    vmem = pl.BlockSpec(memory_space=pltpu.VMEM)
    both = 2 * rows
    return pl.pallas_call(
        functools.partial(feed_kernel, chunks),
        out_shape=(
            jax.ShapeDtypeStruct((rows, width), BF),
            jax.ShapeDtypeStruct((rows, width), F32),
            jax.ShapeDtypeStruct((slices, width, units), BF),
            jax.ShapeDtypeStruct((slices, width, units), BF),
            jax.ShapeDtypeStruct((slices, 1, units), F32),
            jax.ShapeDtypeStruct((8, width), F32),
        ),
        in_specs=[vmem] * 6,
        out_specs=[vmem] * 6,
        scratch_shapes=[
            pltpu.VMEM((both, width), BF),
            pltpu.VMEM((slices, both, units), BF),
            pltpu.VMEM((slices, both, units), BF),
            pltpu.VMEM((slices, both, units), BF),
            pltpu.VMEM((both, width), BF),
            pltpu.VMEM((rows, width), F32),
            pltpu.VMEM((rows, width), F32),
            pltpu.VMEM((2, rows, width), BF),
            pltpu.VMEM((2, rows, width), BF),
            pltpu.SemaphoreType.DMA((4, chunks)),
            pltpu.SemaphoreType.DMA((4, chunks)),
        ],
        compiler_params=pltpu.CompilerParams(
            collective_id=1, has_side_effects=True, vmem_limit_bytes=VMEM_LIMIT
        ),
    )(attended, cotangent, expand, shrink, expand_offset, vectors)


def product(left, right):
    return jnp.dot(left, right, preferred_element_type=F32)


def product_rows(left, right):
    return lax.dot_general(left, right, TN, preferred_element_type=F32)


def product_last(left, right):
    return lax.dot_general(left, right, NT, preferred_element_type=F32)


def attend_forward(queries, key_rows, values, block_rows):
    length, heads_here, head_size = queries.shape
    block_count = length // block_rows

    def one_block(query_block):
        scores = jnp.einsum("qhd,khd->hqk", query_block, key_rows, preferred_element_type=F32)
        largest = jnp.max(scores, axis=-1, keepdims=True)
        weights = jnp.exp(scores - largest)
        exp_total = jnp.sum(weights, axis=-1, keepdims=True)
        probs_low = (weights / exp_total).astype(BF)
        mixture = jnp.einsum("hqk,khd->qhd", probs_low, values, preferred_element_type=F32)
        log_total = (largest + jnp.log(exp_total))[..., 0]
        return (mixture.astype(BF), log_total)

    mixture, log_totals = lax.map(
        one_block, queries.reshape(block_count, block_rows, heads_here, head_size)
    )
    return (mixture.reshape(length, heads_here * head_size), log_totals)


def attend_backward(queries, key_rows, values, mixture_low, log_totals, block_rows):
    length, heads_here, head_size = queries.shape
    block_count = length // block_rows

    def one_block(accumulated, inputs):
        key_sum, value_sum = accumulated
        query_block, grad_block, log_block = inputs
        scores = jnp.einsum("qhd,khd->hqk", query_block, key_rows, preferred_element_type=F32)
        probability = jnp.exp(scores - log_block[..., None])
        probs_low = probability.astype(BF)
        value_sum = value_sum + jnp.einsum(
            "hqk,qhd->khd", probs_low, grad_block, preferred_element_type=F32
        )
        prob_grad = jnp.einsum("qhd,khd->hqk", grad_block, values, preferred_element_type=F32)
        inner_sum = jnp.sum(prob_grad * probability, axis=-1, keepdims=True)
        score_low = (probability * (prob_grad - inner_sum)).astype(BF)
        query_low = jnp.einsum("hqk,khd->qhd", score_low, key_rows, preferred_element_type=F32)
        key_sum = key_sum + jnp.einsum(
            "hqk,qhd->khd", score_low, query_block, preferred_element_type=F32
        )
        return ((key_sum, value_sum), query_low.astype(BF))

    zeros = jnp.zeros((length, heads_here, head_size), F32)
    blocked = (length // block_count, heads_here, head_size)
    (key_sum, value_sum), query_low = lax.scan(
        one_block,
        (zeros, zeros),
        (
            queries.reshape((block_count,) + blocked),
            mixture_low.reshape((block_count,) + blocked),
            log_totals,
        ),
    )
    width_here = heads_here * head_size
    return (
        query_low.reshape(length, width_here),
        key_sum.astype(BF).reshape(length, width_here),
        value_sum.astype(BF).reshape(length, width_here),
    )


def scatter_sum(partial, axis):
    return lax.psum_scatter(
        partial.astype(BF), "dp", scatter_dimension=axis, tiled=True
    ).astype(F32)


def body(
    layer_input,
    query_weight,
    key_weight,
    value_weight,
    mixing_weight,
    expand_weight,
    shrink_weight,
    query_offset,
    value_offset,
    mixing_offset,
    expand_offset,
    shrink_offset,
    first_gain,
    first_shift,
    second_gain,
    second_shift,
    cotangent,
):
    local_rows = layer_input.shape[0]
    tensor_size = lax.axis_size("tensor")
    length = local_rows * tensor_size
    block_rows = min(512, length)
    heads_here = query_weight.shape[1] // HD
    scaling = HD ** (-0.5)
    head_shape = (length, heads_here, HD)
    swap = [(i, i ^ 2) for i in range(tensor_size)]

    def pair(shard):
        return jnp.stack([shard, lax.ppermute(shard, "tensor", swap)])

    query_full = lax.all_gather(query_weight, "dp", axis=0, tiled=True)
    key_full = lax.all_gather(key_weight, "dp", axis=0, tiled=True)
    value_full = lax.all_gather(value_weight, "dp", axis=0, tiled=True)
    mixing_full = lax.all_gather(mixing_weight, "dp", axis=1, tiled=True)
    expand_full = lax.all_gather(pair(expand_weight), "dp", axis=1, tiled=True)
    shrink_full = lax.all_gather(pair(shrink_weight.T), "dp", axis=1, tiled=True)
    offset_pair = pair(expand_offset.astype(F32)[None, :])
    sequence = lax.all_gather(layer_input, "tensor", axis=0, tiled=True)
    queries = ((product(sequence, query_full) + query_offset.astype(F32)) * scaling).astype(BF)
    key_rows = product(sequence, key_full).astype(BF)
    values = (product(sequence, value_full) + value_offset.astype(F32)).astype(BF)
    mixture, log_totals = attend_forward(
        queries.reshape(head_shape),
        key_rows.reshape(head_shape),
        values.reshape(head_shape),
        block_rows,
    )
    attended_part = lax.psum_scatter(
        product(mixture, mixing_full).astype(BF), "tensor", scatter_dimension=0, tiled=True
    )
    attended = layer_input.astype(F32) + attended_part + mixing_offset.astype(F32)
    zero = jnp.zeros_like(first_gain)
    vectors = jnp.stack(
        [first_gain, first_shift, second_gain, second_shift, shrink_offset, zero, zero, zero]
    ).astype(F32)
    output, attended_grad, expand_local, shrink_local, expand_sum, sums = feed_forward(
        attended, cotangent, expand_full, shrink_full, offset_pair, vectors
    )
    attended_rows = lax.all_gather(attended_grad.astype(BF), "tensor", axis=0, tiled=True)
    mixing_local = product_rows(mixture, attended_rows)
    mixture_low = product_last(attended_rows, mixing_full).astype(BF)
    query_low, key_low, value_low = attend_backward(
        queries.reshape(head_shape),
        key_rows.reshape(head_shape),
        values.reshape(head_shape),
        mixture_low,
        log_totals,
        block_rows,
    )
    query_local = product_rows(sequence, query_low) * scaling
    key_local = product_rows(sequence, key_low)
    value_local = product_rows(sequence, value_low)
    query_sum = jnp.sum(query_low.astype(F32), axis=0) * scaling
    value_sum = jnp.sum(value_low.astype(F32), axis=0)
    input_grad = (
        lax.psum_scatter(
            (
                product_last(query_low, query_full) * scaling
                + product_last(key_low, key_full)
                + product_last(value_low, value_full)
            ).astype(BF),
            "tensor",
            scatter_dimension=0,
            tiled=True,
        ).astype(F32)
        + attended_grad
    )
    query_grad = scatter_sum(query_local, 0)
    key_grad = scatter_sum(key_local, 0)
    value_grad = scatter_sum(value_local, 0)
    mixing_grad = scatter_sum(mixing_local, 1)
    expand_parts = lax.psum_scatter(expand_local, "dp", scatter_dimension=1, tiled=True)
    shrink_parts = lax.psum_scatter(shrink_local, "dp", scatter_dimension=1, tiled=True)

    def join(parts):
        theirs = lax.ppermute(parts[1], "tensor", swap)
        return parts[0].astype(F32) + theirs.astype(F32)

    expand_grad = join(expand_parts)
    shrink_grad = join(shrink_parts).T
    tensor_index = lax.axis_index("tensor")

    def spread_out(vector, index):
        selector = (jnp.arange(tensor_size)[:, None] == index).astype(F32)
        return (selector * vector[None, :]).reshape(-1)

    totals = lax.psum(
        (
            sums,
            spread_out(query_sum, tensor_index),
            spread_out(value_sum, tensor_index),
            spread_out(expand_sum[0, 0], tensor_index)
            + spread_out(expand_sum[1, 0], tensor_index ^ 2),
        ),
        ("dp", "tensor"),
    )

    def own_slice(full_vector, slice_size):
        return lax.dynamic_slice_in_dim(full_vector, tensor_index * slice_size, slice_size, 0)

    offset_query = own_slice(totals[1], query_sum.shape[0])
    offset_value = own_slice(totals[2], value_sum.shape[0])
    offset_expand = own_slice(totals[3], expand_offset.shape[0])
    sums = totals[0]
    return (
        output,
        input_grad,
        query_grad,
        key_grad,
        value_grad,
        mixing_grad,
        expand_grad,
        shrink_grad,
        offset_query,
        offset_value,
        sums[5],
        offset_expand,
        sums[2],
        sums[3],
        sums[4],
        sums[0],
        sums[1],
    )


def solution(mesh):
    rows = P(("dp", "tensor"), None)
    tall = P("dp", "tensor")
    wide = P("tensor", "dp")
    split = P("tensor")
    whole = P()
    return jax.shard_map(
        body,
        mesh=mesh,
        in_specs=(rows, tall, tall, tall, wide, tall, wide, split, split)
        + (whole, split, whole, whole, whole, whole, whole, rows),
        out_specs=(rows, rows, tall, tall, tall, wide, tall, wide, split, split)
        + (whole, split, whole, whole, whole, whole, whole),
        check_vma=False,
    )
```

time: 714 us -> 575 us (0.81)
  waiting for transfers between devices: 446 us -> 302 us
  Pallas kernels: 0 us -> 56.3 us
  matrix products: 99.2 us -> 52 us
    reduce_scatter x5 -> x4, waiting for transfers between devices: 203 us -> 40.2 us  [the longest x1 40.2 us: body(): lax.psum_scatter((product_last(query_low, query_full) * scaling + product...]
    ppermute x0 -> x5, waiting for transfers between devices: none -> 56.3 us  [the longest x3 56.3 us: pair(): return jnp.stack([shard, lax.ppermute(shard, 'tensor', swap)])]
    pallas_call x0 -> x1, Pallas kernels: none -> 56.3 us  [feed_forward(): pl.pallas_call(functools.partial(feed_kernel, chunks), out_shape=(jax.Sha...]
    all_gather x5 -> x3, waiting for transfers between devices: 134 us -> 86.4 us  [the longest x1 44.4 us: body(): lax.all_gather(attended_grad.astype(BF), 'tensor', axis=0, tiled=True)]
    dot_general x24 -> x18, matrix products: 88.2 us -> 41 us  [the longest x4 10.4 us: product_rows(): return lax.dot_general(left, right, TN, preferred_element_type=F32)]
    reduce_sum x11 -> x2, other arithmetic: 11.9 us -> 0.29 us  [the longest x1 0.15 us: body(): query_sum = jnp.sum(query_low.astype(F32), axis=0) * scaling]
    unnamed x21 -> x16, waiting for transfers between devices: 101 us -> 110 us
    unnamed x71 -> x72, local copies, waits for them, and re-layouts: 21.5 us -> 17.8 us
  transfers between devices with their start and end apart: 16 -> 17, of which waited for: 13 -> 11; matrix products, arithmetic and copies ran while one was open for 14% -> 13% of each run, Pallas kernels for 0% -> 0%
where the time goes in v2:
time: 575 us; the launch traced here: 565 us
  waiting for transfers between devices  302 us (53%)
  blocking collectives  79.2 us (14%)
  Pallas kernels  56.3 us (10%)
  matrix products  52 us (9%)
  local copies, waits for them, and re-layouts  31.1 us (5%)
  other arithmetic  22.7 us (4%)
  between operations  16.6 us (3%)
    unnamed x16, waiting for transfers between devices  110 us
    ppermute x3, waiting for transfers between devices, pair(): return jnp.stack([shard, lax.ppermute(shard, 'tensor', swap)])  56.3 us
    pallas_call x1, Pallas kernels, feed_forward(): pl.pallas_call(functools.partial(feed_kernel, chunks), out_shape=(jax.Sha...  56.3 us
    all_gather x1, waiting for transfers between devices, body(): lax.all_gather(attended_grad.astype(BF), 'tensor', axis=0, tiled=True)  44.4 us
    reduce_scatter x1, waiting for transfers between devices, body(): lax.psum_scatter((product_last(query_low, query_full) * scaling + product...  40.2 us
    psum x1, blocking collectives, body(): lax.psum((sums, spread_out(query_sum, tensor_index), spread_out(value_sum...  39.3 us
    all_gather x1, waiting for transfers between devices, body(): expand_full = lax.all_gather(pair(expand_weight), 'dp', axis=1, tiled=True)  39.1 us
    unnamed x72, local copies, waits for them, and re-layouts  17.8 us
  transfers between devices with their start and end apart: 17, of which 11 were waited for; matrix products, arithmetic and copies ran while one was open for 13% of the time, Pallas kernels for 0%

profile of v2, /device:TPU:0, one launch (start us, length us, event | category | flops | bytes accessed | tf_op | source)
XLA Modules:
  0.0 565.1 jit_solution(7649318618215867992)
XLA Ops:
  10.1 11.6 %all_gather.25 = bf16[1024,256]{1,0:T(8,128)(2,1)S(1)} all-gather(bf16[128,256]{1,0:T(8,128)(2,1)} %param.22), channel_id=1, replica_groups=mesh['dp'=8,'tensor'=4] {'dp'}, dimensions={0}, use_global_device_ids=true | all-gather | bytes 589824 | tf_op jit(solution)/shard_map/all_gather | solution.py:395
  21.7 9.5 %all_gather.26 = bf16[1024,256]{1,0:T(8,128)(2,1)S(1)} all-gather(bf16[128,256]{1,0:T(8,128)(2,1)} %param.23), channel_id=1, replica_groups=mesh['dp'=8,'tensor'=4] {'dp'}, dimensions={0}, use_global_device_ids=true | all-gather | bytes 589824 | tf_op jit(solution)/shard_map/all_gather | solution.py:396
  31.3 9.2 %all_gather.27 = bf16[1024,256]{1,0:T(8,128)(2,1)S(1)} all-gather(bf16[128,256]{1,0:T(8,128)(2,1)} %param.24), channel_id=1, replica_groups=mesh['dp'=8,'tensor'=4] {'dp'}, dimensions={0}, use_global_device_ids=true | all-gather | bytes 589824 | tf_op jit(solution)/shard_map/all_gather | solution.py:397
  40.4 9.6 %all_gather.28 = bf16[256,1024]{1,0:T(8,128)(2,1)S(1)} all-gather(bf16[256,128]{1,0:T(8,128)(2,1)} %param.25), channel_id=1, replica_groups=mesh['dp'=8,'tensor'=4] {'dp'}, dimensions={1}, use_global_device_ids=true | all-gather | bytes 589824 | tf_op jit(solution)/shard_map/all_gather | solution.py:398
  50.1 9.0 %all-gather.5.cloned.1.call-done = bf16[1024,1024]{1,0:T(8,128)(2,1)} async-done(((bf16[256,1024]{1,0:T(8,128)(2,1)}), bf16[1024,1024]{1,0:T(8,128)(2,1)}) %all-gather.5.cloned.1.call-update) | async-done | bytes 2097168 | tf_op jit(solution)/shard_map/all_gather | solution.py:402
  59.1 3.1 fusion.37
  64.9 2.3 convolution_convert_fusion.6
  67.2 2.3 fusion.38
  69.6 10.2 %while.27 = (s32[]{:T(128)}, bf16[2,512,4,64]{1,3,2,0:T(8,128)(2,1)S(1)}, f32[2,4,512]{2,1,0:T(4,128)S(1)}, bf16[2,512,4,64]{1,3,2,0:T(8,128)(2,1)S(1)}, bf16[10...) while((s32[]{:T(128)}, bf16[2,512,4,64]{1,3,2,0:T(8,128)(2,1)S(1)}, ...), condition=%wide.region_3.4_spmd, body=%wide.region_0.3_spmd.sunk | while | flops 549582848 | bytes 26804320 | solution.py:311
  84.1 30.2 %collective-permute-done.1 = bf16[128,1024]{1,0:T(8,128)(2,1)S(1)} collective-permute-done((bf16[128,1024]{1,0:T(8,128)(2,1)S(1)}, bf16[128,1024]{1,0:T(8,128)(2,1)S(1)}, u32[]{:S(2)}, u32[]{:S(2)}) %collective-permute-start.1) | collective-permute-done | bytes 262176 | tf_op jit(solution)/shard_map/ppermute | solution.py:393
  115.3 22.5 %collective-permute-done = bf16[128,1024]{1,0:T(8,128)(2,1)S(1)} collective-permute-done((bf16[128,1024]{1,0:T(8,128)(2,1)}, bf16[128,1024]{1,0:T(8,128)(2,1)S(1)}, u32[]{:S(2)}, u32[]{:S(2)}) %collective-permute-start) | collective-permute-done | bytes 262176 | tf_op jit(solution)/shard_map/ppermute | solution.py:393
  140.5 3.7 collective-permute-done.2
  147.0 2.9 all-gather.9.cloned.1.call-done.shrink_ref
  149.9 39.1 %all-gather.7.cloned.1.call-done.expand_ref = bf16[2,1024,1024]{2,1,0:T(8,128)(2,1)} async-done(((bf16[2,128,1024]{2,1,0:T(8,128)(2,1)}), bf16[2,1024,1024]{2,1,0:T(8,128)(2,1)}) %all-gather.7.cloned.1.call-update) | async-done | bytes 4194320 | tf_op jit(solution)/shard_map/all_gather | solution.py:399
  189.0 56.3 %shard_map.296 = (bf16[256,1024]{1,0:T(8,128)(2,1)}, f32[256,1024]{1,0:T(8,128)}, bf16[2,1024,1024]{2,1,0:T(8,128)(2,1)}, bf16[2,1024,1024]{2,1,0:T(8,128)(2,1)}...) custom-call(f32[256,1024]{1,0:T(8,128)} %add_add_fusion.attended_ref, bf16[256,1024]{1,0:T(8,128)(2,1)} %cotangent_ref.1, ...), custom_call_target="tpu_custom_call" | custom-call | tf_op jit(solution)/shard_map/pallas_call | solution.py:254
  249.0 44.4 %all-gather.11.cloned.1.call-done = bf16[1024,1024]{1,0:T(8,128)(2,1)} async-done(((bf16[256,1024]{1,0:T(8,128)(2,1)}), bf16[1024,1024]{1,0:T(8,128)(2,1)}) %all-gather.11.cloned.1.call-update) | async-done | bytes 2097168 | tf_op jit(solution)/shard_map/all_gather | solution.py:423
  293.4 3.4 convolution_convert_fusion.2
  298.9 3.2 convolution_convert_fusion.5
  302.1 2.8 reshape.144
  304.8 2.3 copy.60
  308.0 19.9 %while.28 = (s32[]{:T(128)}, f32[1024,4,64]{0,2,1:T(8,128)S(1)}, f32[1024,4,64]{0,2,1:T(8,128)S(1)}, bf16[2,512,4,64]{1,3,2,0:T(8,128)(2,1)}, bf16[2,512,4,64]{1...) while((s32[]{:T(128)}, f32[1024,4,64]{0,2,1:T(8,128)S(1)}, ...), condition=%wide.region_7.8_spmd.clone, body=%wide.region_5.7_spmd.clone.sunk | while | flops 1362229248 | bytes 78438664 | solution.py:341
  311.2 2.6 multiply_reduce_fusion.2
  321.1 2.6 multiply_reduce_fusion.2
  330.6 2.3 fusion.40
  334.0 2.4 fusion.41
  337.6 2.3 fusion.42
  341.0 2.8 fusion.48
  349.0 39.3 %all-reduce = (f32[1024]{0:T(1024)S(1)}, f32[1024]{0:T(1024)S(1)}, f32[8,1024]{1,0:T(8,128)S(1)}, f32[4096]{0:T(1024)S(1)}) all-reduce(f32[1024]{0:T(1024)S(1)} %bitcast.198, f32[1024]{0:T(1024)S(1)} %bitcast.197, f32[8,1024]{1,0:T(8,128)S(1)} %copy-done.21, f32[4096]{0:T(1024)S(1)} %bitcast.195), channel_id=1, replica_groups=mesh['dp'=8,'tensor'=4] {'dp','tensor'}, use_global_device_ids=true, to_apply=%region_16.17 | all-reduce | flops 14336 | bytes 114688 | tf_op jit(solution)/shard_map/psum | solution.py:471
  397.5 36.0 %reduce-scatter.25.cloned.1.call-done = bf16[128,256]{1,0:T(8,128)(2,1)} async-done(((bf16[1024,256]{1,0:T(8,128)(2,1)}), bf16[128,256]{1,0:T(8,128)(2,1)}) %reduce-scatter.25.cloned.1.call-update) | async-done | bytes 65552
  435.2 36.2 %reduce-scatter.27.cloned.1.call-done = bf16[128,256]{1,0:T(8,128)(2,1)} async-done(((bf16[1024,256]{1,0:T(8,128)(2,1)}), bf16[128,256]{1,0:T(8,128)(2,1)}) %reduce-scatter.27.cloned.1.call-update) | async-done | bytes 65552
  473.2 35.4 %reduce-scatter.29.cloned.1.call-done = bf16[128,256]{1,0:T(8,128)(2,1)} async-done(((bf16[1024,256]{1,0:T(8,128)(2,1)}), bf16[128,256]{1,0:T(8,128)(2,1)}) %reduce-scatter.29.cloned.1.call-update) | async-done | bytes 65552
  514.1 40.2 %reduce-scatter.19.cloned.1.call-done = bf16[256,1024]{1,0:T(8,128)(2,1)} async-done(((bf16[1024,1024]{1,0:T(8,128)(2,1)}), bf16[256,1024]{1,0:T(8,128)(2,1)}) %reduce-scatter.19.cloned.1.call-update) | async-done | bytes 524304 | tf_op jit(solution)/shard_map/reduce_scatter | solution.py:440
  (192 shorter events, 78.7 us)
Async XLA Ops:
  8.0 51.1 %all-gather.5.cloned.1.call-start = ((), (), s32[]{:S(2)}) async-start(), calls=%async_computation.8 | async-start | bytes 2621440 | tf_op jit(solution)/shard_map/all_gather | solution.py:402
  8.8 136.0 %reduce-scatter.17.cloned.1.call-start = ((), (), s32[]{:S(2)}) async-start(), calls=%async_computation.9 | async-start | bytes 2621440 | tf_op jit(solution)/shard_map/reduce_scatter | solution.py:412
  21.7 40.5 %copy-start.10 = (bf16[1024,256]{1,0:T(8,128)(2,1)}, bf16[1024,256]{1,0:T(8,128)(2,1)S(1)}, u32[]{:S(2)}) copy-start(bf16[1024,256]{1,0:T(8,128)(2,1)S(1)} %all_gather.25) | copy-start | bytes 1572868
  31.2 33.6 %copy-start.12 = (bf16[1024,256]{1,0:T(8,128)(2,1)}, bf16[1024,256]{1,0:T(8,128)(2,1)S(1)}, u32[]{:S(2)}) copy-start(bf16[1024,256]{1,0:T(8,128)(2,1)S(1)} %all_gather.26) | copy-start | bytes 1572868
  50.1 30.4 %copy-start.17 = (bf16[256,1024]{1,0:T(8,128)(2,1)}, bf16[256,1024]{1,0:T(8,128)(2,1)S(1)}, u32[]{:S(2)}) copy-start(bf16[256,1024]{1,0:T(8,128)(2,1)S(1)} %all_gather.28) | copy-start | bytes 1572868
  79.9 35.2 %copy-start.2 = (bf16[1024,4,64]{0,2,1:T(8,128)(2,1)}, bf16[1024,4,64]{0,2,1:T(8,128)(2,1)S(1)}, u32[]{:S(2)}) copy-start(bf16[1024,4,64]{0,2,1:T(8,128)(2,1)S(1)} %get-tuple-element.496) | copy-start | bytes 1572868
  80.5 59.0 %copy-start.18 = (bf16[32,8,2,512]{3,1,2,0:T(8,128)(2,1)}, bf16[32,8,2,512]{3,1,2,0:T(8,128)(2,1)S(1)}, u32[]{:S(2)}) copy-start(bf16[32,8,2,512]{3,1,2,0:T(8,128)(2,1)S(1)} %copy.78) | copy-start | bytes 1572868
  80.5 59.1 %copy-start.23 = (bf16[1024]{0:T(1024)(128)(2,1)S(1)}, bf16[1024]{0:T(1024)(128)(2,1)}, u32[]{:S(2)}) copy-start(bf16[1024]{0:T(1024)(128)(2,1)} %param.31) | copy-start | bytes 6148
  80.5 59.2 %copy-start.24 = (bf16[1024]{0:T(1024)(128)(2,1)S(1)}, bf16[1024]{0:T(1024)(128)(2,1)}, u32[]{:S(2)}) copy-start(bf16[1024]{0:T(1024)(128)(2,1)} %param.30) | copy-start | bytes 6148
  80.5 59.2 %copy-start.25 = (bf16[1024]{0:T(1024)(128)(2,1)S(1)}, bf16[1024]{0:T(1024)(128)(2,1)}, u32[]{:S(2)}) copy-start(bf16[1024]{0:T(1024)(128)(2,1)} %param.32) | copy-start | bytes 6148
  80.6 59.2 %copy-start.26 = (bf16[1024]{0:T(1024)(128)(2,1)S(1)}, bf16[1024]{0:T(1024)(128)(2,1)}, u32[]{:S(2)}) copy-start(bf16[1024]{0:T(1024)(128)(2,1)} %param.33) | copy-start | bytes 6148
  80.6 59.2 %copy-start.27 = (bf16[1024]{0:T(1024)(128)(2,1)S(1)}, bf16[1024]{0:T(1024)(128)(2,1)}, u32[]{:S(2)}) copy-start(bf16[1024]{0:T(1024)(128)(2,1)} %param.34) | copy-start | bytes 6148
  80.6 59.2 %copy-start.28 = (bf16[1024]{0:T(1024)(128)(2,1)S(1)}, bf16[1024]{0:T(1024)(128)(2,1)}, u32[]{:S(2)}) copy-start(bf16[1024]{0:T(1024)(128)(2,1)} %param.35) | copy-start | bytes 6148
  80.6 59.2 %copy-start.29 = (bf16[1024]{0:T(1024)(128)(2,1)S(1)}, bf16[1024]{0:T(1024)(128)(2,1)}, u32[]{:S(2)}) copy-start(bf16[1024]{0:T(1024)(128)(2,1)} %param.36) | copy-start | bytes 6148
  80.6 64.2 %copy-start.16 = (bf16[256,1024]{1,0:T(8,128)(2,1)S(1)}, bf16[256,1024]{1,0:T(8,128)(2,1)}, u32[]{:S(2)}) copy-start(bf16[256,1024]{1,0:T(8,128)(2,1)} %param.21) | copy-start | bytes 1572868
  82.7 67.2 %all-gather.9.cloned.1.call-start = ((), (), s32[]{:S(2)}) async-start(), calls=%async_computation.11 | async-start | bytes 4718592 | tf_op jit(solution)/shard_map/all_gather | solution.py:400
  83.0 31.3 %collective-permute-start.1 = (bf16[128,1024]{1,0:T(8,128)(2,1)S(1)}, bf16[128,1024]{1,0:T(8,128)(2,1)S(1)}, u32[]{:S(2)}, u32[]{:S(2)}) collective-permute-start(bf16[128,1024]{1,0:T(8,128)(2,1)S(1)} %bitcast.190), channel_id=1, source_target_pairs={{0,2},{1,3},{2,0},{3,1},{4,6},{5,7},{6,4},{7,5},{8,10},{9,11},{10,... | collective-permute-start | bytes 786440 | tf_op jit(solution)/shard_map/ppermute | solution.py:393
  115.1 73.9 %all-gather.7.cloned.1.call-start = ((), (), s32[]{:S(2)}) async-start(), calls=%async_computation.10 | async-start | bytes 4718592 | tf_op jit(solution)/shard_map/all_gather | solution.py:399
  115.2 22.5 %collective-permute-start = (bf16[128,1024]{1,0:T(8,128)(2,1)}, bf16[128,1024]{1,0:T(8,128)(2,1)S(1)}, u32[]{:S(2)}, u32[]{:S(2)}) collective-permute-start(bf16[128,1024]{1,0:T(8,128)(2,1)} %param.26), channel_id=1, source_target_pairs={{0,2},{1,3},{2,0},{3,1},{4,6},{5,7},{6,4},{7,5},{8,10},{9,11},{10,... | collective-permute-start | bytes 786440 | tf_op jit(solution)/shard_map/ppermute | solution.py:393
  139.5 153.9 %all-gather.11.cloned.1.call-start = ((), (), s32[]{:S(2)}) async-start(), calls=%async_computation.12 | async-start | bytes 2621440 | tf_op jit(solution)/shard_map/all_gather | solution.py:423
  139.6 4.6 collective-permute-start.2
  247.4 140.9 %reduce-scatter.23.cloned.1.call-start = ((), (), s32[]{:S(2)}) async-start(), calls=%async_computation.15 | async-start | bytes 4718592 | tf_op jit(solution)/shard_map/reduce_scatter | solution.py:457
  248.0 143.6 %reduce-scatter.21.cloned.1.call-start = ((), (), s32[]{:S(2)}) async-start(), calls=%async_computation.14 | async-start | bytes 4718592 | tf_op jit(solution)/shard_map/reduce_scatter | solution.py:456
  248.8 147.1 %reduce-scatter.31.cloned.1.call-start = ((), (), s32[]{:S(2)}) async-start(), calls=%async_computation.19 | async-start | bytes 589824
  307.1 126.3 %reduce-scatter.25.cloned.1.call-start = ((), (), s32[]{:S(2)}) async-start(), calls=%async_computation.16 | async-start | bytes 589824
  333.9 137.6 %reduce-scatter.27.cloned.1.call-start = ((), (), s32[]{:S(2)}) async-start(), calls=%async_computation.17 | async-start | bytes 589824
  337.4 171.1 %reduce-scatter.29.cloned.1.call-start = ((), (), s32[]{:S(2)}) async-start(), calls=%async_computation.18 | async-start | bytes 589824
  343.8 210.5 %reduce-scatter.19.cloned.1.call-start = ((), (), s32[]{:S(2)}) async-start(), calls=%async_computation.13 | async-start | bytes 2621440 | tf_op jit(solution)/shard_map/reduce_scatter | solution.py:440
  348.5 205.9 %copy-start.7 = (f32[256,1024]{1,0:T(8,128)S(1)}, f32[256,1024]{1,0:T(8,128)}, u32[]{:S(2)}) copy-start(f32[256,1024]{1,0:T(8,128)} %get-tuple-element.108) | copy-start | bytes 3145732
  348.8 207.7 %copy-start.19 = (bf16[256,1024]{1,0:T(8,128)(2,1)S(1)}, bf16[256,1024]{1,0:T(8,128)(2,1)}, u32[]{:S(2)}) copy-start(bf16[256,1024]{1,0:T(8,128)(2,1)} %get-tuple-element.465) | copy-start | bytes 1572868
  389.4 120.9 %collective-permute-start.4 = (bf16[128,1024]{1,0:T(8,128)(2,1)S(1)}, bf16[128,1024]{1,0:T(8,128)(2,1)S(1)}, u32[]{:S(2)}, u32[]{:S(2)}) collective-permute-start(bf16[128,1024]{1,0:T(8,128)(2,1)S(1)} %slice_bitcast_fusion), channel_id=1, source_target_pairs={{0,2},{1,3},{2,0},{3,1},{4,6},{5,7},{6,4},{7,5},{8,10},{9,11},{10,... | collective-permute-start | bytes 786440 | tf_op jit(solution)/shard_map/ppermute | solution.py:460
  392.6 119.7 %collective-permute-start.3 = (bf16[128,1024]{1,0:T(8,128)(2,1)S(1)}, bf16[128,1024]{1,0:T(8,128)(2,1)S(1)}, u32[]{:S(2)}, u32[]{:S(2)}) collective-permute-start(bf16[128,1024]{1,0:T(8,128)(2,1)S(1)} %slice_bitcast_fusion.2), channel_id=1, source_target_pairs={{0,2},{1,3},{2,0},{3,1},{4,6},{5,7},{6,4},{7,5},{8,10},{9,11},{10,... | collective-permute-start | bytes 786440 | tf_op jit(solution)/shard_map/ppermute | solution.py:460
  (19 other events, 68.6 us)
Sparse Core Ops, SparseCore 0:
  10.4 48.6 all-gather.4
  82.9 56.4 reduce-scatter.16
  247.6 45.8 all-gather.10
Sparse Core Ops, SparseCore 1:
  115.2 34.7 all-gather.8
  152.5 36.5 all-gather.6
  251.6 51.1 reduce-scatter.22
  306.1 51.6 reduce-scatter.20
  361.2 34.4 reduce-scatter.30
  399.3 34.1 reduce-scatter.24
  437.3 34.1 reduce-scatter.26
  474.4 34.1 reduce-scatter.28
  510.8 43.4 reduce-scatter.18

commit v3 on v2

--- a/solution.py
+++ b/solution.py
@@ -57,20 +57,135 @@
     lax.fori_loop(0, width // step, one, 0)
 
 
-def feed_kernel(
+def chosen(table, index):
+    value = jnp.int32(table[0])
+    for place in range(1, len(table)):
+        value = jnp.where(index == place, jnp.int32(table[place]), value)
+    return value
+
+
+def each(count, start, body):
+    if count - start <= 8:
+        for index in range(start, count):
+            body(index)
+        return
+
+    def one(index, carry):
+        body(index)
+        return carry
+
+    lax.fori_loop(start, count, one, 0)
+
+
+class Place:
+    def __init__(self, devices, ranks):
+        self.d = lax.axis_index("dp")
+        self.t = lax.axis_index("tensor")
+        self.chips = devices // 2
+        self.ranks = ranks
+        self.c = self.d % 2
+        self.p = self.d // 2
+
+    def chip(self, k):
+        return {"dp": 2 * (self.p ^ k) + self.c}
+
+    def core(self):
+        return {"dp": self.d ^ 1}
+
+    def rank(self, t):
+        return {"tensor": t}
+
+
+def remote(source, target, sems, index, device):
+    send, recv = sems
+    return pltpu.make_async_remote_copy(
+        src_ref=source,
+        dst_ref=target,
+        send_sem=send.at[index],
+        recv_sem=recv.at[index],
+        device_id=device,
+        device_id_type=MESH,
+    )
+
+
+class Gather:
+    def __init__(self, here, view, chip_sems, core_sems):
+        self.here, self.view = here, view
+        self.chip_sems, self.core_sems = chip_sems, core_sems
+
+    def chip_copy(self, k):
+        here = self.here
+        mine = self.view(2 * here.p + here.c)
+        return remote(mine, mine, self.chip_sems, k, here.chip(k))
+
+    def chip_arrival(self, k):
+        here = self.here
+        theirs = self.view(2 * (here.p ^ k) + here.c)
+        return remote(theirs, theirs, self.chip_sems, k, here.chip(k))
+
+    def core_copy(self, k):
+        here = self.here
+        shard = self.view(2 * (here.p ^ k) + here.c)
+        return remote(shard, shard, self.core_sems, k, here.core())
+
+    def core_arrival(self, k):
+        here = self.here
+        shard = self.view(2 * (here.p ^ k) + 1 - here.c)
+        return remote(shard, shard, self.core_sems, k, here.core())
+
+    def start(self):
+        each(self.here.chips, 1, lambda k: self.chip_copy(k).start())
+        self.core_copy(0).start()
+
+    def forward(self):
+        def one(k):
+            self.chip_arrival(k).wait_recv()
+            self.core_copy(k).start()
+
+        each(self.here.chips, 1, one)
+
+    def finish(self):
+        each(self.here.chips, 0, lambda k: self.core_arrival(k).wait_recv())
+
+    def drain(self):
+        each(self.here.chips, 1, lambda k: self.chip_copy(k).wait_send())
+        each(self.here.chips, 0, lambda k: self.core_copy(k).wait_send())
+
+
+def layer_kernel(
+    devices,
     chunks,
-    attended_ref,
-    cotangent_ref,
+    input_ref,
+    query_ref,
+    key_ref,
+    value_ref,
+    mixing_ref,
     expand_ref,
     shrink_ref,
+    head_offset_ref,
     expand_offset_ref,
     vectors_ref,
+    cotangent_ref,
     output_ref,
     attended_grad_ref,
     expand_grad_ref,
     shrink_grad_ref,
     expand_sum_ref,
     sums_ref,
+    sequence,
+    queries,
+    key_rows,
+    values,
+    mixed,
+    log_totals,
+    head_full,
+    mixing_full,
+    feed_full,
+    offset_full,
+    key_columns,
+    value_columns,
+    mix_heads,
+    attended_ref,
     normed,
     hidden,
     slope,
@@ -80,64 +195,285 @@
     summed_grad,
     send_part,
     recv_part,
-    send_sem,
-    recv_sem,
+    row_send,
+    row_recv,
+    mix_send,
+    mix_recv,
+    weight_send,
+    weight_recv,
+    pair_send,
+    pair_recv,
+    chip_send,
+    chip_recv,
+    core_send,
+    core_recv,
+    swap_send,
+    swap_recv,
 ):
-    rows, width = attended_ref.shape
-    slices, _, units = expand_ref.shape
+    ranks, rows, width = sequence.shape
+    shard = query_ref.shape[0]
+    span = query_ref.shape[1]
+    heads = span // HD
+    units = expand_ref.shape[1]
+    slices = 2
     step = rows // chunks
-    t = lax.axis_index("tensor")
-    partner = {"tensor": t ^ 1}
+    length = ranks * rows
+    here = Place(devices, ranks)
+    d, t, chips = here.d, here.t, here.chips
+    last = ranks - 1
+    middle = jnp.logical_and(t > 0, t < last)
+    partner = here.rank(t ^ 1)
     first_gain = vectors_ref[0:1, :]
     first_shift = vectors_ref[1:2, :]
     second_gain = vectors_ref[2:3, :]
     second_shift = vectors_ref[3:4, :]
     shrink_offset = vectors_ref[4:5, :]
+    mixing_offset = vectors_ref[5:6, :]
+
+    barrier = pltpu.get_barrier_semaphore()
+    for k in range(1, ranks):
+        pl.semaphore_signal(barrier, inc=1, device_id=here.rank(t ^ k), device_id_type=MESH)
+    each(
+        chips,
+        1,
+        lambda k: pl.semaphore_signal(
+            barrier, inc=1, device_id=here.chip(k), device_id_type=MESH
+        ),
+    )
+    pl.semaphore_signal(barrier, inc=1, device_id=here.core(), device_id_type=MESH)
+
+    mine = pl.ds(pl.multiple_of(d * shard, shard), shard)
+    sequence[t] = input_ref[...]
+    head_full[0, mine, :] = query_ref[...]
+    head_full[1, mine, :] = key_ref[...]
+    head_full[2, mine, :] = value_ref[...]
+    mixing_full[t, mine, :] = mixing_ref[...]
+    feed_full[0, 0, mine, :] = expand_ref[...]
+    feed_full[0, 1, mine, :] = shrink_ref[...]
+    offset_full[0] = expand_offset_ref[...]
+
+    pl.semaphore_wait(barrier, ranks - 1 + chips - 1 + 1)
+
+    def shard_rows(index):
+        return pl.ds(pl.multiple_of(index * shard, shard), shard)
+
+    def gather(number, view):
+        return Gather(
+            here,
+            view,
+            (chip_send.at[number], chip_recv.at[number]),
+            (core_send.at[number], core_recv.at[number]),
+        )
+
+    heads_gather = gather(0, lambda i: head_full.at[:, shard_rows(i)])
+    mixing_gather = gather(1, lambda i: mixing_full.at[:, shard_rows(i)])
+    feed_gathers = [
+        gather(2 + s, lambda i, s=s: feed_full.at[s, :, shard_rows(i)]) for s in range(slices)
+    ]
+
+    row_sems = (row_send, row_recv)
+
+    def row_copy(s, side):
+        block = sequence.at[s]
+        return pltpu.make_async_remote_copy(
+            src_ref=block,
+            dst_ref=block,
+            send_sem=row_send.at[side, s],
+            recv_sem=row_recv.at[s],
+            device_id=here.rank(jnp.clip(t + (1 if side else -1), 0, last)),
+            device_id_type=MESH,
+        )
+
+    @pl.when(t < last)
+    def _():
+        row_copy(t, 1).start()
+
+    @pl.when(t > 0)
+    def _():
+        row_copy(t, 0).start()
+
+    heads_gather.start()
+    heads_gather.forward()
+    feed_gathers[0].start()
+    heads_gather.finish()
+
+    def project(s):
+        block = sequence[s]
+        place = pl.ds(pl.multiple_of(s * rows, rows), rows)
+        query = (mm(block, head_full[0], NN) + head_offset_ref[0:1, :]) * (HD**-0.5)
+        queries[s] = query.astype(BF)
+        key = mm(block, head_full[1], NN)
+        key_rows[place, :] = key.astype(BF)
+        value = mm(block, head_full[2], NN) + head_offset_ref[1:2, :]
+        values[place, :] = value.astype(BF)
+        value_columns[:, place] = value.T.astype(BF)
+        key_columns[:, place] = key.T.astype(BF)
+
+    project(t)
+
+    def weight_copy(k):
+        return remote(
+            mixing_full.at[t, mine],
+            mixing_full.at[t, mine],
+            (weight_send, weight_recv),
+            k,
+            here.rank(t ^ k),
+        )
+
+    def weight_arrival(k):
+        theirs = mixing_full.at[t ^ k, mine]
+        return remote(theirs, theirs, (weight_send, weight_recv), k, here.rank(t ^ k))
+
+    pair_copies = [
+        remote(
+            feed_full.at[0, :, mine],
+            feed_full.at[1, :, mine],
+            (pair_send, pair_recv),
+            0,
+            here.rank(t ^ 2),
+        ),
+        remote(
+            offset_full.at[0], offset_full.at[1], (pair_send, pair_recv), 1, here.rank(t ^ 2)
+        ),
+    ]
+
+    def start_pairs():
+        for k in range(1, ranks):
+            weight_copy(k).start()
+        for copy in pair_copies:
+            copy.start()
+
+    near = [
+        [s for _, s in sorted((abs(s - u), s) for s in range(ranks) if s != u)]
+        for u in range(ranks)
+    ]
+    for j in range(ranks - 1):
+        s = chosen([near[u][j] for u in range(ranks)], t)
+        row_copy(s, 0).wait_recv()
+
+        @pl.when(jnp.logical_and(s < t, t < last))
+        def _():
+            row_copy(s, 1).start()
+
+        @pl.when(jnp.logical_and(s > t, t > 0))
+        def _():
+            row_copy(s, 0).start()
+
+        if j == 1:
+
+            @pl.when(jnp.logical_not(middle))
+            def _():
+                start_pairs()
+
+        project(s)
+
+    def mix_copy(s):
+        return pltpu.make_async_remote_copy(
+            src_ref=mix_heads.at[s],
+            dst_ref=mixed.at[t],
+            send_sem=mix_send.at[s],
+            recv_sem=mix_recv.at[t],
+            device_id=here.rank(s),
+            device_id_type=MESH,
+        )
+
+    def mix_arrival(s):
+        return pltpu.make_async_remote_copy(
+            src_ref=mix_heads.at[s],
+            dst_ref=mixed.at[s],
+            send_sem=mix_send.at[s],
+            recv_sem=mix_recv.at[s],
+            device_id=here.rank(s),
+            device_id_type=MESH,
+        )
+
+    lane = lax.broadcasted_iota(jnp.int32, (1, 128), 1)
+
+    def attend(s):
+        place = pl.ds(pl.multiple_of(s * rows, rows), rows)
+        columns = []
+        for h in range(heads):
+            pair = slice(128 * (h // 2), 128 * (h // 2) + 128)
+            side = (lane // HD) == (h % 2)
+            query = jnp.where(side, queries[s, :, pair], jnp.zeros((), BF))
+            scores = mm(key_rows[:, pair], query, NT)
+            largest = jnp.max(scores, axis=0, keepdims=True)
+            weights = jnp.exp(scores - largest)
+            total = jnp.sum(weights, axis=0, keepdims=True)
+            column = mm(value_columns[h * HD : (h + 1) * HD, :], weights.astype(BF), NN)
+            columns.append(column / total)
+            log_totals[h : h + 1, place] = largest + jnp.log(total)
+        mix_heads[s] = jnp.concatenate(columns, axis=0).T.astype(BF)
+
+    far = [[s for s in reversed(near[u])] + [u] for u in range(ranks)]
+    for j in range(ranks):
+        s = chosen([far[u][j] for u in range(ranks)], t)
+        attend(s)
+        if j < ranks - 1:
+            mix_copy(s).start()
+        if j == 0:
+
+            @pl.when(middle)
+            def _():
+                start_pairs()
+
+        if j == 1:
+            feed_gathers[0].forward()
+    mixed[t] = mix_heads[t]
+
+    for k in range(1, ranks):
+        weight_arrival(k).wait_recv()
+    mixing_gather.start()
+    for copy in pair_copies:
+        copy.wait_recv()
+    feed_gathers[1].start()
+    for k in range(1, ranks):
+        mix_arrival(t ^ k).wait_recv()
+    mixing_gather.forward()
+    mixing_gather.finish()
+
+    def mix_tile(tile):
+        total = input_ref[:, tile].astype(F32) + vectors_ref[5:6, tile]
+        for j in range(ranks):
+            total = total + mm(mixed[j], mixing_full[j, tile, :], NT)
+        attended_ref[:, tile] = total
+
+    tiles(width, mix_tile)
+
+    def own(chunk):
+        return pl.ds(chunk * step, step)
+
+    def other(chunk):
+        return pl.ds(rows + chunk * step, step)
 
     def exchange(kind, chunk, source, target):
         return pltpu.make_async_remote_copy(
             src_ref=source,
             dst_ref=target,
-            send_sem=send_sem.at[kind, chunk],
-            recv_sem=recv_sem.at[kind, chunk],
+            send_sem=swap_send.at[kind, chunk],
+            recv_sem=swap_recv.at[kind, chunk],
             device_id=partner,
             device_id_type=MESH,
         )
 
-    def own(chunk):
-        return pl.ds(chunk * step, step)
-
-    def other(chunk):
-        return pl.ds(rows + chunk * step, step)
-
     copies = [
         [exchange(0, c, normed.at[own(c)], normed.at[other(c)]) for c in range(chunks)],
-        [
-            exchange(1, c, send_part.at[0, own(c)], recv_part.at[0, own(c)])
-            for c in range(chunks)
-        ],
+        [exchange(1, c, send_part.at[0, own(c)], recv_part.at[0, own(c)]) for c in range(chunks)],
         [exchange(2, c, summed_low.at[own(c)], summed_low.at[other(c)]) for c in range(chunks)],
-        [
-            exchange(3, c, send_part.at[1, own(c)], recv_part.at[1, own(c)])
-            for c in range(chunks)
-        ],
+        [exchange(3, c, send_part.at[1, own(c)], recv_part.at[1, own(c)]) for c in range(chunks)],
     ]
-
-    barrier = pltpu.get_barrier_semaphore()
-    pl.semaphore_signal(barrier, inc=1, device_id=partner, device_id_type=MESH)
     for c in range(chunks):
         normal, _ = norm_parts(attended_ref[own(c), :])
         normed[own(c), :] = (normal * first_gain + first_shift).astype(BF)
-    pl.semaphore_wait(barrier, 1)
-    for c in range(chunks):
         copies[0][c].start()
 
-    def forward(place, store):
+    def forward(place, store, ready):
         for s in range(slices):
+            ready(s)
 
             def grow(tile):
-                value = mm(normed[place, :], expand_ref[s, :, tile], NN)
-                value = value + expand_offset_ref[s, :, tile]
+                value = mm(normed[place, :], feed_full[s, 0, :, tile], NN)
+                value = value + offset_full[s, :, tile]
                 share = 0.5 * (1.0 + lax.erf(value * 0.7071067811865476))
                 density = jnp.exp(-0.5 * value * value) * 0.3989422804014327
                 hidden[s, place, tile] = (value * share).astype(BF)
@@ -146,9 +482,9 @@
             tiles(units, grow)
 
         def shrink(tile):
-            total = mm(hidden[0, place, :], shrink_ref[0, tile, :], NT)
+            total = mm(hidden[0, place, :], feed_full[0, 1, tile, :], NT)
             for s in range(1, slices):
-                total = total + mm(hidden[s, place, :], shrink_ref[s, tile, :], NT)
+                total = total + mm(hidden[s, place, :], feed_full[s, 1, tile, :], NT)
             store(tile, total)
 
         tiles(width, shrink)
@@ -157,16 +493,16 @@
         for s in range(slices):
 
             def narrow(tile):
-                value = mm(summed_low[place, :], shrink_ref[s, :, tile], NN)
+                value = mm(summed_low[place, :], feed_full[s, 1, :, tile], NN)
                 value = value * slope[s, place, tile].astype(F32)
                 expanded_low[s, place, tile] = value.astype(BF)
 
             tiles(units, narrow)
 
         def widen(tile):
-            total = mm(expanded_low[0, place, :], expand_ref[0, tile, :], NT)
+            total = mm(expanded_low[0, place, :], feed_full[0, 0, tile, :], NT)
             for s in range(1, slices):
-                total = total + mm(expanded_low[s, place, :], expand_ref[s, tile, :], NT)
+                total = total + mm(expanded_low[s, place, :], feed_full[s, 0, tile, :], NT)
             store(tile, total)
 
         tiles(width, widen)
@@ -180,10 +516,17 @@
 
         return store
 
-    forward(pl.ds(0, rows), keep)
+    def arrive(s):
+        if s == 0:
+            feed_gathers[0].finish()
+        else:
+            feed_gathers[s].forward()
+            feed_gathers[s].finish()
+
+    forward(pl.ds(0, rows), keep, arrive)
     for c in range(chunks):
         copies[0][c].wait_recv()
-        forward(other(c), pass_on(0, c))
+        forward(other(c), pass_on(0, c), lambda s: None)
         copies[1][c].start()
 
     sums_ref[...] = jnp.zeros_like(sums_ref)
@@ -240,30 +583,68 @@
         sums_ref[3:4, :] += column_sum(upstream * normal)
         sums_ref[4:5, :] += column_sum(upstream)
         sums_ref[5:6, :] += column_sum(grad)
+
     for kind in range(4):
         for c in range(chunks):
             copies[kind][c].wait_send()
-
-
-def feed_forward(attended, cotangent, expand, shrink, expand_offset, vectors):
-    rows, width = attended.shape
-    slices, _, units = expand.shape
+    for each_gather in [heads_gather, mixing_gather] + feed_gathers:
+        each_gather.drain()
+    for copy in pair_copies:
+        copy.wait_send()
+    for k in range(1, ranks):
+        weight_copy(k).wait_send()
+        mix_copy(t ^ k).wait_send()
+    for s in range(ranks):
+
+        @pl.when(jnp.logical_and(s <= t, t < last))
+        def _():
+            row_copy(s, 1).wait_send()
+
+        @pl.when(jnp.logical_and(s >= t, t > 0))
+        def _():
+            row_copy(s, 0).wait_send()
+
+
+def layer(devices, ranks, inputs):
+    layer_input = inputs[0]
+    rows, width = layer_input.shape
+    span = inputs[1].shape[1]
+    units = inputs[5].shape[1]
+    slices = 2
     chunks = 2
+    chips = devices // 2
+    length = ranks * rows
+    both = 2 * rows
     vmem = pl.BlockSpec(memory_space=pltpu.VMEM)
-    both = 2 * rows
+    dma = pltpu.SemaphoreType.DMA
+    outs = (
+        jax.ShapeDtypeStruct((rows, width), BF),
+        jax.ShapeDtypeStruct((rows, width), F32),
+        jax.ShapeDtypeStruct((slices, width, units), BF),
+        jax.ShapeDtypeStruct((slices, width, units), BF),
+        jax.ShapeDtypeStruct((slices, 1, units), F32),
+        jax.ShapeDtypeStruct((8, width), F32),
+        jax.ShapeDtypeStruct((ranks, rows, width), BF),
+        jax.ShapeDtypeStruct((ranks, rows, span), BF),
+        jax.ShapeDtypeStruct((length, span), BF),
+        jax.ShapeDtypeStruct((length, span), BF),
+        jax.ShapeDtypeStruct((ranks, rows, span), BF),
+        jax.ShapeDtypeStruct((8, length), F32),
+        jax.ShapeDtypeStruct((3, width, span), BF),
+        jax.ShapeDtypeStruct((ranks, width, span), BF),
+    )
     return pl.pallas_call(
-        functools.partial(feed_kernel, chunks),
-        out_shape=(
-            jax.ShapeDtypeStruct((rows, width), BF),
-            jax.ShapeDtypeStruct((rows, width), F32),
-            jax.ShapeDtypeStruct((slices, width, units), BF),
-            jax.ShapeDtypeStruct((slices, width, units), BF),
-            jax.ShapeDtypeStruct((slices, 1, units), F32),
-            jax.ShapeDtypeStruct((8, width), F32),
-        ),
-        in_specs=[vmem] * 6,
-        out_specs=[vmem] * 6,
+        functools.partial(layer_kernel, devices, chunks),
+        out_shape=outs,
+        in_specs=[vmem] * len(inputs),
+        out_specs=[vmem] * len(outs),
         scratch_shapes=[
+            pltpu.VMEM((slices, 2, width, units), BF),
+            pltpu.VMEM((slices, 1, units), F32),
+            pltpu.VMEM((span, length), BF),
+            pltpu.VMEM((span, length), BF),
+            pltpu.VMEM((ranks, rows, span), BF),
+            pltpu.VMEM((rows, width), F32),
             pltpu.VMEM((both, width), BF),
             pltpu.VMEM((slices, both, units), BF),
             pltpu.VMEM((slices, both, units), BF),
@@ -273,13 +654,25 @@
             pltpu.VMEM((rows, width), F32),
             pltpu.VMEM((2, rows, width), BF),
             pltpu.VMEM((2, rows, width), BF),
-            pltpu.SemaphoreType.DMA((4, chunks)),
-            pltpu.SemaphoreType.DMA((4, chunks)),
+            dma((2, ranks)),
+            dma((ranks,)),
+            dma((ranks,)),
+            dma((ranks,)),
+            dma((ranks,)),
+            dma((ranks,)),
+            dma((2,)),
+            dma((2,)),
+            dma((4, chips)),
+            dma((4, chips)),
+            dma((4, chips)),
+            dma((4, chips)),
+            dma((4, chunks)),
+            dma((4, chunks)),
         ],
         compiler_params=pltpu.CompilerParams(
             collective_id=1, has_side_effects=True, vmem_limit_bytes=VMEM_LIMIT
         ),
-    )(attended, cotangent, expand, shrink, expand_offset, vectors)
+    )(*inputs)
 
 
 def product(left, right):
@@ -382,6 +775,7 @@
 ):
     local_rows = layer_input.shape[0]
     tensor_size = lax.axis_size("tensor")
+    tensor_index = lax.axis_index("tensor")
     length = local_rows * tensor_size
     block_rows = min(512, length)
     heads_here = query_weight.shape[1] // HD
@@ -389,36 +783,49 @@
     head_shape = (length, heads_here, HD)
     swap = [(i, i ^ 2) for i in range(tensor_size)]
 
-    def pair(shard):
-        return jnp.stack([shard, lax.ppermute(shard, "tensor", swap)])
-
-    query_full = lax.all_gather(query_weight, "dp", axis=0, tiled=True)
-    key_full = lax.all_gather(key_weight, "dp", axis=0, tiled=True)
-    value_full = lax.all_gather(value_weight, "dp", axis=0, tiled=True)
-    mixing_full = lax.all_gather(mixing_weight, "dp", axis=1, tiled=True)
-    expand_full = lax.all_gather(pair(expand_weight), "dp", axis=1, tiled=True)
-    shrink_full = lax.all_gather(pair(shrink_weight.T), "dp", axis=1, tiled=True)
-    offset_pair = pair(expand_offset.astype(F32)[None, :])
-    sequence = lax.all_gather(layer_input, "tensor", axis=0, tiled=True)
-    queries = ((product(sequence, query_full) + query_offset.astype(F32)) * scaling).astype(BF)
-    key_rows = product(sequence, key_full).astype(BF)
-    values = (product(sequence, value_full) + value_offset.astype(F32)).astype(BF)
-    mixture, log_totals = attend_forward(
-        queries.reshape(head_shape),
-        key_rows.reshape(head_shape),
-        values.reshape(head_shape),
-        block_rows,
-    )
-    attended_part = lax.psum_scatter(
-        product(mixture, mixing_full).astype(BF), "tensor", scatter_dimension=0, tiled=True
-    )
-    attended = layer_input.astype(F32) + attended_part + mixing_offset.astype(F32)
     zero = jnp.zeros_like(first_gain)
     vectors = jnp.stack(
-        [first_gain, first_shift, second_gain, second_shift, shrink_offset, zero, zero, zero]
+        [first_gain, first_shift, second_gain, second_shift, shrink_offset, mixing_offset, zero, zero]
     ).astype(F32)
-    output, attended_grad, expand_local, shrink_local, expand_sum, sums = feed_forward(
-        attended, cotangent, expand_full, shrink_full, offset_pair, vectors
+    (
+        output,
+        attended_grad,
+        expand_local,
+        shrink_local,
+        expand_sum,
+        sums,
+        sequence,
+        queries,
+        key_rows,
+        values,
+        mixture_own,
+        log_totals,
+        head_full,
+        mixing_full,
+    ) = layer(
+        lax.axis_size("dp"),
+        tensor_size,
+        (
+            layer_input,
+            query_weight,
+            key_weight,
+            value_weight,
+            mixing_weight.T,
+            expand_weight,
+            shrink_weight.T,
+            jnp.stack([query_offset, value_offset]).astype(F32),
+            expand_offset.astype(F32)[None, :],
+            vectors,
+            cotangent,
+        ),
+    )
+    sequence = sequence.reshape(length, -1)
+    queries = queries.reshape(length, -1)
+    query_full, key_full, value_full = head_full[0], head_full[1], head_full[2]
+    mixture = lax.all_to_all(mixture_own, "tensor", 0, 0, tiled=True).reshape(length, -1)
+    mixing_full = mixing_full[tensor_index].T
+    log_totals = jnp.moveaxis(
+        log_totals[:heads_here].reshape(heads_here, length // block_rows, block_rows), 1, 0
     )
     attended_rows = lax.all_gather(attended_grad.astype(BF), "tensor", axis=0, tiled=True)
     mixing_local = product_rows(mixture, attended_rows)
@@ -462,7 +869,6 @@
 
     expand_grad = join(expand_parts)
     shrink_grad = join(shrink_parts).T
-    tensor_index = lax.axis_index("tensor")
 
     def spread_out(vector, index):
         selector = (jnp.arange(tensor_size)[:, None] == index).astype(F32)

time: 575 us -> 497 us (0.86)
  waiting for transfers between devices: 302 us -> 185 us
  Pallas kernels: 56.3 us -> 144 us
  blocking collectives: 79.2 us -> 40.6 us
  matrix products: 52 us -> 42 us
    unnamed x16 -> x9, waiting for transfers between devices: 110 us -> 1.15 us
    reduce_scatter x1 -> x3, waiting for transfers between devices: 0.01 us -> 102 us  [scatter_sum(): lax.psum_scatter(partial.astype(BF), 'dp', scatter_dimension=axis, tiled=...]
    pallas_call x1, Pallas kernels: 56.3 us -> 144 us  [layer(): pl.pallas_call(functools.partial(layer_kernel, devices, chunks), out_shap...]
    ppermute x3 -> x0, waiting for transfers between devices: 56.3 us -> none  [pair(): return jnp.stack([shard, lax.ppermute(shard, 'tensor', swap)])]
    all_gather x3 -> x0, waiting for transfers between devices: 51.1 us -> none  [the longest x1 39.1 us: body(): expand_full = lax.all_gather(pair(expand_weight), 'dp', axis=1, tiled=True)]
    all_gather x4 -> x0, blocking collectives: 39.9 us -> none  [the longest x1 11.6 us: body(): query_full = lax.all_gather(query_weight, 'dp', axis=0, tiled=True)]
    all_gather x1, waiting for transfers between devices: 44.4 us -> 25.8 us  [body(): lax.all_gather(attended_grad.astype(BF), 'tensor', axis=0, tiled=True)]
    all_to_all x0 -> x1, waiting for transfers between devices: none -> 15.8 us  [body(): lax.all_to_all(mixture_own, 'tensor', 0, 0, tiled=True).reshape(length, -1)]
  transfers between devices with their start and end apart: 17 -> 11, of which waited for: 11 -> 6; matrix products, arithmetic and copies ran while one was open for 13% -> 16% of each run, Pallas kernels for 0% -> 0%
where the time goes in v3:
time: 497 us; the launch traced here: 487 us
  waiting for transfers between devices  185 us (37%)
  Pallas kernels  144 us (29%)
  matrix products  42 us (8%)
  blocking collectives  40.6 us (8%)
  local copies, waits for them, and re-layouts  32 us (6%)
  other arithmetic  18.7 us (4%)
  between operations  16.2 us (3%)
  starting transfers between devices  7.96 us (2%)
    pallas_call x1, Pallas kernels, layer(): pl.pallas_call(functools.partial(layer_kernel, devices, chunks), out_shap...  144 us
    reduce_scatter x3, waiting for transfers between devices, scatter_sum(): lax.psum_scatter(partial.astype(BF), 'dp', scatter_dimension=axis, tiled=...  102 us
    psum x1, blocking collectives, body(): lax.psum((sums, spread_out(query_sum, tensor_index), spread_out(value_sum...  40.6 us
    reduce_scatter x1, waiting for transfers between devices, body(): lax.psum_scatter((product_last(query_low, query_full) * scaling + product...  40.4 us
    all_gather x1, waiting for transfers between devices, body(): lax.all_gather(attended_grad.astype(BF), 'tensor', axis=0, tiled=True)  25.8 us
    all_to_all x1, waiting for transfers between devices, body(): lax.all_to_all(mixture_own, 'tensor', 0, 0, tiled=True).reshape(length, -1)  15.8 us
    unnamed x26, local copies, waits for them, and re-layouts  12.8 us
    dot_general x4, matrix products, product_rows(): return lax.dot_general(left, right, TN, preferred_element_type=F32)  12.7 us
  transfers between devices with their start and end apart: 11, of which 6 were waited for; matrix products, arithmetic and copies ran while one was open for 16% of the time, Pallas kernels for 0%

profile of v3, /device:TPU:0, one launch (start us, length us, event | category | flops | bytes accessed | tf_op | source)
XLA Modules:
  0.0 487.2 jit_solution(8736444100864721231)
XLA Ops:
  19.4 144.3 %shard_map.296 = (bf16[256,1024]{1,0:T(8,128)(2,1)}, f32[256,1024]{1,0:T(8,128)}, bf16[2,1024,1024]{2,1,0:T(8,128)(2,1)}, bf16[2,1024,1024]{2,1,0:T(8,128)(2,1)}...) custom-call(bf16[256,1024]{1,0:T(8,128)(2,1)} %input_ref.1, ...), custom_call_target="tpu_custom_call" | custom-call | tf_op jit(solution)/shard_map/pallas_call | solution.py:636
  163.7 2.1 convert_element_type.107
  167.0 4.3 all-to-all-start
  172.6 2.0 copy.59
  174.7 2.8 reshape.125
  177.4 2.3 copy.60
  179.7 15.8 %all-to-all-done = bf16[4,256,256]{2,1,0:T(8,128)(2,1)S(1)} async-done(((bf16[4,256,256]{2,1,0:T(8,128)(2,1)}), bf16[4,256,256]{2,1,0:T(8,128)(2,1)S(1)}, u32[]{:S(2)}, u32[]{:S(2)}) %all-to-all-start) | async-done | bytes 524320 | tf_op jit(solution)/shard_map/all_to_all | solution.py:825
  195.5 25.8 %all-gather.2.cloned.1.call-done = bf16[1024,1024]{1,0:T(8,128)(2,1)} async-done(((bf16[256,1024]{1,0:T(8,128)(2,1)}), bf16[1024,1024]{1,0:T(8,128)(2,1)}) %all-gather.2.cloned.1.call-update) | async-done | bytes 2097168 | tf_op jit(solution)/shard_map/all_gather | solution.py:830
  221.2 3.2 convolution_convert_fusion.1
  224.4 2.1 copy.68
  226.5 2.4 convolution_convert_fusion.4
  231.9 21.8 %while.15 = (s32[]{:T(128)}, f32[1024,4,64]{0,2,1:T(8,128)S(1)}, f32[1024,4,64]{0,2,1:T(8,128)S(1)}, bf16[2,512,4,64]{1,3,2,0:T(8,128)(2,1)}, bf16[2,512,4,64]{1...) while((s32[]{:T(128)}, f32[1024,4,64]{0,2,1:T(8,128)S(1)}, ...), condition=%wide.region_2.3_spmd.clone, body=%wide.region_0.2_spmd.clone.sunk | while | flops 1362229248 | bytes 78438664 | solution.py:734
  231.9 2.2 fusion.81
  234.2 1.8 fusion.83
  236.0 2.6 multiply_reduce_fusion.2
  242.8 2.2 fusion.81
  245.1 1.8 fusion.83
  246.9 2.6 multiply_reduce_fusion.2
  255.4 3.1 fusion.27
  258.9 3.2 convolution_convert_fusion.3
  262.4 3.2 convolution_convert_fusion.2
  265.6 3.8 fusion.30
  269.4 2.0 fusion.32
  272.1 3.2 add_convert_fusion
  275.9 40.6 %all-reduce = (f32[1024]{0:T(1024)S(1)}, f32[1024]{0:T(1024)S(1)}, f32[8,1024]{1,0:T(8,128)S(1)}, f32[4096]{0:T(1024)S(1)}) all-reduce(f32[1024]{0:T(1024)S(1)} %bitcast.155, f32[1024]{0:T(1024)S(1)} %bitcast.154, f32[8,1024]{1,0:T(8,128)S(1)} %copy-done.8, f32[4096]{0:T(1024)S(1)} %bitcast.151), channel_id=1, replica_groups=mesh['dp'=8,'tensor'=4] {'dp','tensor'}, use_global_device_ids=true, to_apply=%region_11.12 | all-reduce | flops 14336 | bytes 114688 | tf_op jit(solution)/shard_map/psum | solution.py:877
  317.5 3.0 collective-permute-start.1
  325.7 29.0 %reduce-scatter.12.cloned.1.call-done = bf16[128,256]{1,0:T(8,128)(2,1)} async-done(((bf16[1024,256]{1,0:T(8,128)(2,1)}), bf16[128,256]{1,0:T(8,128)(2,1)}) %reduce-scatter.12.cloned.1.call-update) | async-done | bytes 65552 | tf_op jit(solution)/shard_map/reduce_scatter | solution.py:752
  356.2 36.3 %reduce-scatter.14.cloned.1.call-done = bf16[128,256]{1,0:T(8,128)(2,1)} async-done(((bf16[1024,256]{1,0:T(8,128)(2,1)}), bf16[128,256]{1,0:T(8,128)(2,1)}) %reduce-scatter.14.cloned.1.call-update) | async-done | bytes 65552 | tf_op jit(solution)/shard_map/reduce_scatter | solution.py:752
  394.0 36.6 %reduce-scatter.16.cloned.1.call-done = bf16[128,256]{1,0:T(8,128)(2,1)} async-done(((bf16[1024,256]{1,0:T(8,128)(2,1)}), bf16[128,256]{1,0:T(8,128)(2,1)}) %reduce-scatter.16.cloned.1.call-update) | async-done | bytes 65552 | tf_op jit(solution)/shard_map/reduce_scatter | solution.py:752
  434.2 1.8 convert_add_fusion.2
  436.0 40.4 %reduce-scatter.10.cloned.1.call-done = bf16[256,1024]{1,0:T(8,128)(2,1)} async-done(((bf16[1024,1024]{1,0:T(8,128)(2,1)}), bf16[256,1024]{1,0:T(8,128)(2,1)}) %reduce-scatter.10.cloned.1.call-update) | async-done | bytes 524304 | tf_op jit(solution)/shard_map/reduce_scatter | solution.py:847
  476.4 2.1 convert_add_fusion
  (111 shorter events, 42.1 us)
Async XLA Ops:
  8.0 213.2 %all-gather.2.cloned.1.call-start = ((), (), s32[]{:S(2)}) async-start(), calls=%async_computation.8 | async-start | bytes 2621440 | tf_op jit(solution)/shard_map/all_gather | solution.py:830
  165.9 150.7 %reduce-scatter.20.cloned.1.call-start = ((), (), s32[]{:S(2)}) async-start(), calls=%async_computation.14 | async-start | bytes 4718592 | tf_op jit(solution)/shard_map/reduce_scatter | solution.py:864
  165.9 5.4 %copy-start.9 = (f32[8,1024]{1,0:T(8,128)S(1)}, f32[8,1024]{1,0:T(8,128)}, u32[]{:S(2)}) copy-start(f32[8,1024]{1,0:T(8,128)} %get-tuple-element.83) | copy-start | bytes 98308
  166.4 154.1 %reduce-scatter.18.cloned.1.call-start = ((), (), s32[]{:S(2)}) async-start(), calls=%async_computation.13 | async-start | bytes 4718592 | tf_op jit(solution)/shard_map/reduce_scatter | solution.py:863
  167.0 28.4 %all-to-all-start = ((bf16[4,256,256]{2,1,0:T(8,128)(2,1)}), bf16[4,256,256]{2,1,0:T(8,128)(2,1)S(1)}, u32[]{:S(2)}, u32[]{:S(2)}) async-start(bf16[4,256,256]{2,1,0:T(8,128)(2,1)} %get-tuple-element.92), calls=%async_computation.4 | async-start | bytes 1048576 | tf_op jit(solution)/shard_map/all_to_all | solution.py:825
  171.3 152.7 %reduce-scatter.22.cloned.1.call-start = ((), (), s32[]{:S(2)}) async-start(), calls=%async_computation.15 | async-start | bytes 589824
  231.8 122.9 %reduce-scatter.12.cloned.1.call-start = ((), (), s32[]{:S(2)}) async-start(), calls=%async_computation.10 | async-start | bytes 589824 | tf_op jit(solution)/shard_map/reduce_scatter | solution.py:752
  234.2 1.8 copy-start
  238.6 1.8 copy-start.4
  240.4 1.4 copy-start.1
  241.8 1.0 copy-start.5
  245.1 1.8 copy-start
  249.5 1.8 copy-start.4
  251.3 1.4 copy-start.1
  252.7 1.0 copy-start.5
  258.6 134.0 %reduce-scatter.14.cloned.1.call-start = ((), (), s32[]{:S(2)}) async-start(), calls=%async_computation.11 | async-start | bytes 589824 | tf_op jit(solution)/shard_map/reduce_scatter | solution.py:752
  262.2 168.5 %reduce-scatter.16.cloned.1.call-start = ((), (), s32[]{:S(2)}) async-start(), calls=%async_computation.12 | async-start | bytes 589824 | tf_op jit(solution)/shard_map/reduce_scatter | solution.py:752
  269.3 207.0 %reduce-scatter.10.cloned.1.call-start = ((), (), s32[]{:S(2)}) async-start(), calls=%async_computation.9 | async-start | bytes 2621440 | tf_op jit(solution)/shard_map/reduce_scatter | solution.py:847
  269.4 2.7 copy-start.2
  272.1 3.3 copy-start.10
  272.1 3.4 copy-start.6
  272.1 3.8 copy-start.8
  275.3 201.0 %copy-start.3 = (f32[256,1024]{1,0:T(8,128)S(1)}, f32[256,1024]{1,0:T(8,128)}, u32[]{:S(2)}) copy-start(f32[256,1024]{1,0:T(8,128)} %get-tuple-element.84) | copy-start | bytes 3145732
  275.5 203.0 %copy-start.7 = (bf16[256,1024]{1,0:T(8,128)(2,1)S(1)}, bf16[256,1024]{1,0:T(8,128)(2,1)}, u32[]{:S(2)}) copy-start(bf16[256,1024]{1,0:T(8,128)(2,1)} %get-tuple-element.352) | copy-start | bytes 1572868
  317.5 114.7 %collective-permute-start.1 = (bf16[128,1024]{1,0:T(8,128)(2,1)S(1)}, bf16[128,1024]{1,0:T(8,128)(2,1)S(1)}, u32[]{:S(2)}, u32[]{:S(2)}) collective-permute-start(bf16[128,1024]{1,0:T(8,128)(2,1)S(1)} %slice_bitcast_fusion), channel_id=1, source_target_pairs={{0,2},{1,3},{2,0},{3,1},{4,6},{5,7},{6,4},{7,5},{8,10},{9,11},{10,... | collective-permute-start | bytes 786440 | tf_op jit(solution)/shard_map/ppermute | solution.py:867
  321.5 112.7 %collective-permute-start = (bf16[128,1024]{1,0:T(8,128)(2,1)S(1)}, bf16[128,1024]{1,0:T(8,128)(2,1)S(1)}, u32[]{:S(2)}, u32[]{:S(2)}) collective-permute-start(bf16[128,1024]{1,0:T(8,128)(2,1)S(1)} %slice_bitcast_fusion.2), channel_id=1, source_target_pairs={{0,2},{1,3},{2,0},{3,1},{4,6},{5,7},{6,4},{7,5},{8,10},{9,11},{10,... | collective-permute-start | bytes 786440 | tf_op jit(solution)/shard_map/ppermute | solution.py:867
Sparse Core Ops, SparseCore 0:
  166.0 55.2 all-gather.1
Sparse Core Ops, SparseCore 1:
  169.7 54.9 reduce-scatter.19
  228.2 51.2 reduce-scatter.17
  282.4 34.1 reduce-scatter.21
  320.5 34.1 reduce-scatter.11
  358.4 34.1 reduce-scatter.13
  396.5 34.1 reduce-scatter.15
  432.8 43.5 reduce-scatter.9
